TPU v7x, 128 devices: a whole 4x4x4 slice. The times are simulated.
128 devices in a mesh: row: 8 (over z_lo, x), col: 16 (over z_hi, y, core).
Axes of the slice: x: 4, y: 4, z: 4 (z_hi: 2, z_lo: 2; z = z_hi * 2 + z_lo), core: 2. Of those that a mesh axis runs over, the one named last changes fastest.
Arguments:
- hessian: float32 [8192, 24576], P('row', 'col'), may hold values from -62 to 62
- block_order: int32 [16, 16], P('col'), may hold values from 0 to 15, each once within a row
- send_slot: int32 [4, 128], P(None, 'col'), may hold values from 0 to 1
Outputs:
- rotated: float32 [8192, 24576], P('row', 'col')
Inputs may be any that keep to these rules, and one draw needn't show every extreme that they name: `block_order`: each row is a permutation.
All inputs are finite; a program needn't handle non-finite values.
Results may differ from a plain program's by a relative error of at most 0.00035.
Values sent between devices are 32-bit elements; how exact they have to be, the bound alone decides.
A program may use at most 128 MiB of HBM per device.

v0:
```python
import jax
import jax.numpy as jnp
from jax import lax
from jax.sharding import PartitionSpec as P

BW = 96
STEPS = 4
INNER = 2


def swapped(value, axis, stride):
    mask = 2**stride
    pairs = [(source, source ^ mask) for source in range(lax.axis_size(axis))]
    return lax.ppermute(value, axis, pairs)


def lower_solve(lower_factor, basis):
    solved = jax.scipy.linalg.solve_triangular(lower_factor, jnp.transpose(basis), lower=True)
    return jnp.transpose(solved)


def rotation(gram_matrix):
    pair_width = gram_matrix.shape[-1]
    scale = jnp.sqrt(jnp.sum(gram_matrix * gram_matrix, axis=(1, 2), keepdims=True))
    current = jnp.broadcast_to(jnp.eye(pair_width, dtype=gram_matrix.dtype), gram_matrix.shape)
    for repeat in range(INNER):
        basis = (
            jnp.einsum("pab,pbc->pac", gram_matrix, current, precision=lax.Precision.HIGHEST)
            / scale
        )
        cross = jnp.einsum("pka,pkb->pab", basis, basis, precision=lax.Precision.HIGHEST)
        factor = jnp.linalg.cholesky(cross)
        current = jax.vmap(lower_solve)(factor, basis)
    return current


def swap_step(pairs, chosen_slots, swap_bit):
    local_rows, pair_count, pair_width = pairs.shape
    slots = pairs.reshape(local_rows, pair_count, 2, pair_width // 2)
    slot_zero = slots[:, :, 0]
    slot_one = slots[:, :, 1]
    chosen = (chosen_slots == 0)[None, :, None]
    outgoing = jnp.where(chosen, slot_zero, slot_one)
    incoming = swapped(outgoing, "col", swap_bit)
    slot_zero = jnp.where(chosen, incoming, slot_zero)
    slot_one = jnp.where(chosen, slot_one, incoming)
    return jnp.stack([slot_zero, slot_one], axis=2).reshape(local_rows, pair_count, pair_width)


def body(hessian, block_order, send_slot):
    local_rows, local_cols = hessian.shape
    row_count = lax.axis_size("row")
    col_bits = lax.axis_size("col").bit_length() - 1
    row_index = lax.axis_index("row")
    blocks = hessian.reshape(local_rows, local_cols // BW, BW)
    blocks = jnp.take(blocks, block_order[0], axis=1)
    local_pairs = blocks.reshape(local_rows, row_count, 2 * BW)
    full_pairs = lax.all_to_all(local_pairs, "row", split_axis=1, concat_axis=0, tiled=True)
    own_sends = lax.dynamic_slice_in_dim(send_slot, row_index, 1, 1)
    for step_index in range(STEPS):
        gram_matrix = jnp.einsum(
            "rpa,rpb->pab", full_pairs, full_pairs, precision=lax.Precision.HIGHEST
        )
        rotator = rotation(gram_matrix)
        full_pairs = jnp.einsum(
            "rpa,pab->rpb", full_pairs, rotator, precision=lax.Precision.HIGHEST
        )
        full_pairs = swap_step(full_pairs, own_sends[step_index], step_index % col_bits)
    result = lax.all_to_all(full_pairs, "row", split_axis=0, concat_axis=1, tiled=True)
    return result.reshape(local_rows, local_cols)


def solution(mesh):
    in_specs = (P("row", "col"), P("col", None), P(None, "col"))
    out_specs = P("row", "col")
    return jax.shard_map(body, mesh=mesh, in_specs=in_specs, out_specs=out_specs, check_vma=False)
```

profile of v0, /device:TPU:0, one launch (start us, length us, event | category | flops | bytes accessed | tf_op | source)
XLA Modules:
  0.0 983.2 jit_solution(8383920020647598735)
XLA Ops:
  28.7 70.7 %all-to-all-done = f32[1024,8,192]{0,2,1:T(8,128)} async-done(((f32[1024,8,192]{0,2,1:T(8,128)}), f32[1024,8,192]{0,2,1:T(8,128)}, u32[]{:S(2)}, u32[]{:S(2)}) %all-to-all-start) | async-done | bytes 6291488 | tf_op jit(solution)/shard_map/all_to_all | solution.py:58
  99.4 10.4 %multiply_reduce_fusion.3 = (f32[]{:T(128)}, f32[192,192]{1,0:T(8,128)S(1)}) fusion(f32[1024,8,192]{0,2,1:T(8,128)} %all-to-all-done), kind=kOutput, calls=%fused_computation.141 | convolution fusion | flops 3623952384 | bytes 6438916 | tf_op jit(solution)/shard_map/rpa,rpb->pab/dot_general | solution.py:61
  111.5 11.7 %custom-call.41 = f32[1,128,128]{2,1,0:T(8,128)S(1)} custom-call(f32[1,128,128]{2,1,0:T(8,128)S(1)} %cholesky.697), custom_call_target="Cholesky" | custom-call | tf_op jit(solution)/shard_map/jit(cholesky)/cholesky | solution.py:32
  142.2 19.7 %custom-call.44 = f32[1,2,128,128]{2,3,1,0:T(8,128)S(1)} custom-call(f32[1,2,128,128]{3,2,1,0:T(8,128)S(1)} %pad_maximum_fusion.4), custom_call_target="InvertDiagBlocksLowerTriangular" | custom-call | tf_op jit(solution)/shard_map/vmap(jit(_solve_triangular))/triangular_solve | solution.py:18
  163.6 11.7 %custom-call.45 = f32[1,128,128]{2,1,0:T(8,128)S(1)} custom-call(f32[1,128,128]{2,1,0:T(8,128)S(1)} %cholesky.700), custom_call_target="Cholesky" | custom-call | tf_op jit(solution)/shard_map/jit(cholesky)/cholesky | solution.py:32
  194.1 19.9 %custom-call.48 = f32[1,2,128,128]{2,3,1,0:T(8,128)S(1)} custom-call(f32[1,2,128,128]{3,2,1,0:T(8,128)S(1)} %pad_maximum_fusion.5), custom_call_target="InvertDiagBlocksLowerTriangular" | custom-call | tf_op jit(solution)/shard_map/vmap(jit(_solve_triangular))/triangular_solve | solution.py:18
  239.6 11.7 %custom-call.49 = f32[1,128,128]{2,1,0:T(8,128)S(1)} custom-call(f32[1,128,128]{2,1,0:T(8,128)S(1)} %cholesky.703), custom_call_target="Cholesky" | custom-call | tf_op jit(solution)/shard_map/jit(cholesky)/cholesky | solution.py:32
  270.2 19.7 %custom-call.52 = f32[1,2,128,128]{2,3,1,0:T(8,128)S(1)} custom-call(f32[1,2,128,128]{3,2,1,0:T(8,128)S(1)} %pad_maximum_fusion.6), custom_call_target="InvertDiagBlocksLowerTriangular" | custom-call | tf_op jit(solution)/shard_map/vmap(jit(_solve_triangular))/triangular_solve | solution.py:18
  291.7 11.7 %custom-call.53 = f32[1,128,128]{2,1,0:T(8,128)S(1)} custom-call(f32[1,128,128]{2,1,0:T(8,128)S(1)} %cholesky.706), custom_call_target="Cholesky" | custom-call | tf_op jit(solution)/shard_map/jit(cholesky)/cholesky | solution.py:32
  322.2 20.1 %custom-call.56 = f32[1,2,128,128]{2,3,1,0:T(8,128)S(1)} custom-call(f32[1,2,128,128]{3,2,1,0:T(8,128)S(1)} %pad_maximum_fusion.7), custom_call_target="InvertDiagBlocksLowerTriangular" | custom-call | tf_op jit(solution)/shard_map/vmap(jit(_solve_triangular))/triangular_solve | solution.py:18
  353.6 67.9 %collective-permute-done.1 = f32[8192,1,96]{0,2,1:T(8,128)S(1)} collective-permute-done((f32[8192,1,96]{0,2,1:T(8,128)S(1)}, f32[8192,1,96]{0,2,1:T(8,128)S(1)}, u32[]{:S(2)}, u32[]{:S(2)}) %collective-permute-start.1) | collective-permute-done | bytes 3145760 | tf_op jit(solution)/shard_map/ppermute | solution.py:14
  430.4 11.7 %custom-call.57 = f32[1,128,128]{2,1,0:T(8,128)S(1)} custom-call(f32[1,128,128]{2,1,0:T(8,128)S(1)} %cholesky.709), custom_call_target="Cholesky" | custom-call | tf_op jit(solution)/shard_map/jit(cholesky)/cholesky | solution.py:32
  461.2 19.7 %custom-call.60 = f32[1,2,128,128]{2,3,1,0:T(8,128)S(1)} custom-call(f32[1,2,128,128]{3,2,1,0:T(8,128)S(1)} %pad_maximum_fusion.8), custom_call_target="InvertDiagBlocksLowerTriangular" | custom-call | tf_op jit(solution)/shard_map/vmap(jit(_solve_triangular))/triangular_solve | solution.py:18
  482.7 11.7 %custom-call.61 = f32[1,128,128]{2,1,0:T(8,128)S(1)} custom-call(f32[1,128,128]{2,1,0:T(8,128)S(1)} %cholesky.712), custom_call_target="Cholesky" | custom-call | tf_op jit(solution)/shard_map/jit(cholesky)/cholesky | solution.py:32
  513.4 20.1 %custom-call.64 = f32[1,2,128,128]{2,3,1,0:T(8,128)S(1)} custom-call(f32[1,2,128,128]{3,2,1,0:T(8,128)S(1)} %pad_maximum_fusion.9), custom_call_target="InvertDiagBlocksLowerTriangular" | custom-call | tf_op jit(solution)/shard_map/vmap(jit(_solve_triangular))/triangular_solve | solution.py:18
  546.4 67.1 %collective-permute-done.2 = f32[8192,1,96]{0,2,1:T(8,128)S(1)} collective-permute-done((f32[8192,1,96]{0,2,1:T(8,128)S(1)}, f32[8192,1,96]{0,2,1:T(8,128)S(1)}, u32[]{:S(2)}, u32[]{:S(2)}) %collective-permute-start.2) | collective-permute-done | bytes 3145760 | tf_op jit(solution)/shard_map/ppermute | solution.py:14
  622.0 11.7 %custom-call.65 = f32[1,128,128]{2,1,0:T(8,128)S(1)} custom-call(f32[1,128,128]{2,1,0:T(8,128)S(1)} %cholesky.715), custom_call_target="Cholesky" | custom-call | tf_op jit(solution)/shard_map/jit(cholesky)/cholesky | solution.py:32
  652.7 19.7 %custom-call.68 = f32[1,2,128,128]{2,3,1,0:T(8,128)S(1)} custom-call(f32[1,2,128,128]{3,2,1,0:T(8,128)S(1)} %pad_maximum_fusion.10), custom_call_target="InvertDiagBlocksLowerTriangular" | custom-call | tf_op jit(solution)/shard_map/vmap(jit(_solve_triangular))/triangular_solve | solution.py:18
  674.2 11.7 %custom-call.69 = f32[1,128,128]{2,1,0:T(8,128)S(1)} custom-call(f32[1,128,128]{2,1,0:T(8,128)S(1)} %cholesky.718), custom_call_target="Cholesky" | custom-call | tf_op jit(solution)/shard_map/jit(cholesky)/cholesky | solution.py:32
  704.7 19.9 %custom-call.72 = f32[1,2,128,128]{2,3,1,0:T(8,128)S(1)} custom-call(f32[1,2,128,128]{3,2,1,0:T(8,128)S(1)} %pad_maximum_fusion.11), custom_call_target="InvertDiagBlocksLowerTriangular" | custom-call | tf_op jit(solution)/shard_map/vmap(jit(_solve_triangular))/triangular_solve | solution.py:18
  737.2 66.7 %collective-permute-done.3 = f32[8192,1,96]{0,2,1:T(8,128)S(1)} collective-permute-done((f32[8192,1,96]{0,2,1:T(8,128)S(1)}, f32[8192,1,96]{0,2,1:T(8,128)S(1)}, u32[]{:S(2)}, u32[]{:S(2)}) %collective-permute-start.3) | collective-permute-done | bytes 3145760 | tf_op jit(solution)/shard_map/ppermute | solution.py:14
  807.7 18.0 %copy.144 = f32[8192,1,192]{2,1,0:T(1,128)} copy(f32[8192,1,192]{0,2,1:T(8,128)} %bitcast.677) | data formatting | bytes 12582912 | tf_op jit(solution)/shard_map/reshape | solution.py:47
  825.7 118.3 %all_to_all.30 = f32[8192,1,192]{2,1,0:T(1,128)} all-to-all(f32[8192,1,192]{2,1,0:T(1,128)} %copy.144), channel_id=1, replica_groups=mesh['row'=8,'col'=16] {'row'}, dimensions={0} | all-to-all | bytes 12582912 | tf_op jit(solution)/shard_map/all_to_all | solution.py:69
  944.0 17.6 %copy.145 = f32[8192,1,192]{0,2,1:T(8,128)} copy(f32[8192,1,192]{2,1,0:T(1,128)} %all_to_all.30) | data formatting | bytes 12582912 | tf_op jit(solution)/shard_map/all_to_all | solution.py:69
  (229 shorter events, 277.5 us)
Async XLA Ops:
  0.0 27.5 %copy-start = (s32[4,8]{1,0:T(4,128)S(1)}, s32[4,8]{1,0:T(4,128)}, u32[]{:S(2)}) copy-start(s32[4,8]{1,0:T(4,128)} %param.8) | copy-start | bytes 388
  21.7 77.7 %all-to-all-start = ((f32[1024,8,192]{0,2,1:T(8,128)}), f32[1024,8,192]{0,2,1:T(8,128)}, u32[]{:S(2)}, u32[]{:S(2)}) async-start(f32[1024,8,192]{0,2,1:T(8,128)} %broadcast_select_fusion), calls=%async_computation | async-start | bytes 12582912 | tf_op jit(solution)/shard_map/all_to_all | solution.py:58
  224.8 6.1 collective-permute-start
  232.1 5.8 copy-start.3
  351.3 70.2 %collective-permute-start.1 = (f32[8192,1,96]{0,2,1:T(8,128)S(1)}, f32[8192,1,96]{0,2,1:T(8,128)S(1)}, u32[]{:S(2)}, u32[]{:S(2)}) collective-permute-start(f32[8192,1,96]{0,2,1:T(8,128)S(1)} %fusion.3), channel_id=1, source_target_pairs={{0,2},{1,3},{2,0},{3,1},{4,6},{5,7},{6,4},{7,5},{8,10},{9,11},{10,... | collective-permute-start | bytes 9437192 | tf_op jit(solution)/shard_map/ppermute | solution.py:14
  422.7 5.9 copy-start.4
  542.5 70.9 %collective-permute-start.2 = (f32[8192,1,96]{0,2,1:T(8,128)S(1)}, f32[8192,1,96]{0,2,1:T(8,128)S(1)}, u32[]{:S(2)}, u32[]{:S(2)}) collective-permute-start(f32[8192,1,96]{0,2,1:T(8,128)S(1)} %fusion.4), channel_id=1, source_target_pairs={{0,4},{1,5},{2,6},{3,7},{4,0},{5,1},{6,2},{7,3},{8,12},{9,13},{10,... | collective-permute-start | bytes 9437192 | tf_op jit(solution)/shard_map/ppermute | solution.py:14
  614.6 5.8 copy-start.2
  733.6 70.3 %collective-permute-start.3 = (f32[8192,1,96]{0,2,1:T(8,128)S(1)}, f32[8192,1,96]{0,2,1:T(8,128)S(1)}, u32[]{:S(2)}, u32[]{:S(2)}) collective-permute-start(f32[8192,1,96]{0,2,1:T(8,128)S(1)} %fusion.5), channel_id=1, source_target_pairs={{0,8},{1,9},{2,10},{3,11},{4,12},{5,13},{6,14},{7,15},{8,0},{9,1},... | collective-permute-start | bytes 9437192 | tf_op jit(solution)/shard_map/ppermute | solution.py:14
  976.1 6.6 copy-start.1
where the time goes:
time: 995 us; the launch traced here: 983 us
  other arithmetic  407 us (41%)
  waiting for transfers between devices  277 us (28%)
  blocking collectives  118 us (12%)
  local copies, waits for them, and re-layouts  75.6 us (8%)
  matrix products  73.4 us (7%)
  between operations  16.7 us (2%)
  starting transfers between devices  14.8 us (1%)
    another operation x56, other arithmetic, rotation(): factor = jnp.linalg.cholesky(cross)  230 us
    ppermute x4, waiting for transfers between devices, swapped(): return lax.ppermute(value, axis, pairs)  207 us
    another operation x34, other arithmetic, lower_solve(): jax.scipy.linalg.solve_triangular(lower_factor, jnp.transpose(basis), low...  160 us
    all_to_all x1, blocking collectives, body(): lax.all_to_all(full_pairs, 'row', split_axis=0, concat_axis=1, tiled=True)  118 us
    all_to_all x1, waiting for transfers between devices, body(): lax.all_to_all(local_pairs, 'row', split_axis=1, concat_axis=0, tiled=True)  70.7 us
    dot_general x4, matrix products, body(): jnp.einsum('rpa,pab->rpb', full_pairs, rotator, precision=lax.Precision.H...  30.1 us
    dot_general x4, matrix products, body(): jnp.einsum('rpa,rpb->pab', full_pairs, full_pairs, precision=lax.Precisio...  27.9 us
    all_to_all x2, local copies, waits for them, and re-layouts, body(): lax.all_to_all(full_pairs, 'row', split_axis=0, concat_axis=1, tiled=True)  23.9 us
  transfers between devices with their start and end apart: 5, of which 5 were waited for; matrix products, arithmetic and copies ran while one was open for 0% of the time, Pallas kernels for 0%

commit v1 on v0

--- a/solution.py
+++ b/solution.py
@@ -1,6 +1,8 @@
 import jax
 import jax.numpy as jnp
 from jax import lax
+from jax.experimental import pallas as pl
+from jax.experimental.pallas import tpu as pltpu
 from jax.sharding import PartitionSpec as P
 
 BW = 96
@@ -14,24 +16,87 @@
     return lax.ppermute(value, axis, pairs)
 
 
-def lower_solve(lower_factor, basis):
-    solved = jax.scipy.linalg.solve_triangular(lower_factor, jnp.transpose(basis), lower=True)
-    return jnp.transpose(solved)
+F32=jnp.float32; BF=jnp.bfloat16
+W=192
+def pieces(x):
+    h=x.astype(BF); r=x-h.astype(F32); m=r.astype(BF); l=(r-m.astype(F32)).astype(BF)
+    return h,m,l
+def outer(left, right):
+    a0,a1,a2=pieces(left); b0,b1,b2=pieces(right)
+    a=jnp.concatenate([a2,a0,a1,a1,a0,a0],0)
+    b=jnp.concatenate([b0,b2,b1,b0,b1,b0],0)
+    return lax.dot_general(a,b,(((0,),(0,)),((),())),preferred_element_type=F32)
+def rsqrt(d):
+    r=lax.rsqrt(d)
+    return r*(1.5-0.5*d*r*r)
+def eliminate(rows, base, NB):
+    diag=rows[0][:,base:base+NB]
+    cols=[jnp.broadcast_to(diag[:,c:c+1],(NB,128)) for c in range(NB)]
+    idx=lax.broadcasted_iota(jnp.int32,(NB,128),0)
+    rows=[[r[:,i:i+128] for i in range(0,r.shape[1],128)] for r in rows]
+    for c in range(NB):
+        col=cols[c]
+        r=rsqrt(jnp.broadcast_to(col[c:c+1],(NB,128)))
+        l=col*r
+        lm=jnp.where(idx>c,l,0.0)
+        for q in range(c+1,NB):
+            cols[q]=cols[q]-lm*jnp.broadcast_to(l[q:q+1],(NB,128))
+        for g in rows:
+            for i in range(len(g)):
+                u=jnp.broadcast_to(g[i][c:c+1],(NB,128))*r
+                g[i]=jnp.where(idx==c,u,g[i]-lm*u)
+    return [jnp.concatenate(g,1) if len(g)>1 else g[0] for g in rows]
+def factor(a_ref, e_ref, NB):
+    for t in range(W//NB):
+        j=t*NB
+        lo=(j//128)*128
+        panel=[a_ref[j:j+NB,lo:]]
+        if e_ref is not None: panel.append(e_ref[j:j+NB,:])
+        out=eliminate(panel,j-lo,NB)
+        u=out[0]
+        ri=lax.broadcasted_iota(jnp.int32,u.shape,0)+(j-lo)
+        ci=lax.broadcasted_iota(jnp.int32,u.shape,1)
+        u=jnp.where(ci>=ri,u,0.0)
+        a_ref[j:j+NB,lo:]=u
+        if lo: a_ref[j:j+NB,:lo]=jnp.zeros((NB,lo),F32)
+        if e_ref is not None: e_ref[j:j+NB,:]=out[1]
+        rem=W-j-NB
+        if rem==0: break
+        left=u[:,j+NB-lo:W-lo]
+        a_ref[j+NB:W,lo:]=a_ref[j+NB:W,lo:]-outer(left,u)
+        if e_ref is not None:
+            e_ref[j+NB:W,:]=e_ref[j+NB:W,:]-outer(left,out[1])
+def rotate(g, a_ref, e_ref, NB):
+    s=jnp.sum(jnp.sum(g*g,axis=0,keepdims=True),axis=1,keepdims=True)
+    y=g/jnp.sqrt(s)
+    yy=y[:,:W]
+    a_ref[:,:W]=lax.dot_general(yy,yy,(((0,),(0,)),((),())),precision=lax.Precision.HIGHEST,preferred_element_type=F32)
+    a_ref[:,W:]=jnp.zeros((W,256-W),F32)
+    factor(a_ref,None,NB)
+    u=a_ref[...]
+    e_ref[...]=u
+    uu=u[:,:W]
+    a_ref[:,:W]=lax.dot_general(uu,uu,(((1,),(1,)),((),())),precision=lax.Precision.HIGHEST,preferred_element_type=F32)
+    a_ref[:,W:]=jnp.zeros((W,256-W),F32)
+    factor(a_ref,e_ref,NB)
+
+def rotation_kernel(gram_ref, turn_ref, a_ref, e_ref):
+    a_ref[...] = jnp.zeros((W, 256), F32)
+    a_ref[:, :W] = gram_ref[0]
+    rotate(a_ref[...], a_ref, e_ref, 32)
+    turn_ref[0] = e_ref[:, :W]
 
 
 def rotation(gram_matrix):
-    pair_width = gram_matrix.shape[-1]
-    scale = jnp.sqrt(jnp.sum(gram_matrix * gram_matrix, axis=(1, 2), keepdims=True))
-    current = jnp.broadcast_to(jnp.eye(pair_width, dtype=gram_matrix.dtype), gram_matrix.shape)
-    for repeat in range(INNER):
-        basis = (
-            jnp.einsum("pab,pbc->pac", gram_matrix, current, precision=lax.Precision.HIGHEST)
-            / scale
-        )
-        cross = jnp.einsum("pka,pkb->pab", basis, basis, precision=lax.Precision.HIGHEST)
-        factor = jnp.linalg.cholesky(cross)
-        current = jax.vmap(lower_solve)(factor, basis)
-    return current
+    return pl.pallas_call(
+        rotation_kernel,
+        out_shape=jax.ShapeDtypeStruct((1, W, W), F32),
+        in_specs=[pl.BlockSpec(memory_space=pltpu.VMEM)],
+        out_specs=pl.BlockSpec(memory_space=pltpu.VMEM),
+        scratch_shapes=[pltpu.VMEM((W, 256), F32), pltpu.VMEM((W, 256), F32)],
+        compiler_params=pltpu.CompilerParams(vmem_limit_bytes=16 * 2**20),
+        name="rotation",
+    )(gram_matrix)
 
 
 def swap_step(pairs, chosen_slots, swap_bit):
@@ -63,7 +128,7 @@
         )
         rotator = rotation(gram_matrix)
         full_pairs = jnp.einsum(
-            "rpa,pab->rpb", full_pairs, rotator, precision=lax.Precision.HIGHEST
+            "rpa,pba->rpb", full_pairs, rotator, precision=lax.Precision.HIGHEST
         )
         full_pairs = swap_step(full_pairs, own_sends[step_index], step_index % col_bits)
     result = lax.all_to_all(full_pairs, "row", split_axis=0, concat_axis=1, tiled=True)

time: 995 us -> 616 us (0.62)
  other arithmetic: 407 us -> 16.6 us
  Pallas kernels: 0 us -> 49.1 us
  matrix products: 73.4 us -> 50.2 us
  between operations: 16.7 us -> 3.26 us
    another operation x90 -> x0, other arithmetic: 390 us -> none  [the longest x56 230 us: rotation(): factor = jnp.linalg.cholesky(cross)]
    pallas_call x0 -> x4, Pallas kernels: none -> 49.1 us  [rotation(): pl.pallas_call(rotation_kernel, out_shape=jax.ShapeDtypeStruct((1, W, W),...]
    dot_general x20 -> x4, matrix products: 37 us -> 24.8 us  [body(): jnp.einsum('rpa,pba->rpb', full_pairs, rotator, precision=lax.Precision.H...]
where the time goes in v1:
time: 616 us; the launch traced here: 604 us
  waiting for transfers between devices  277 us (45%)
  blocking collectives  118 us (19%)
  local copies, waits for them, and re-layouts  74.5 us (12%)
  matrix products  50.2 us (8%)
  Pallas kernels  49.1 us (8%)
  other arithmetic  16.6 us (3%)
  starting transfers between devices  15.2 us (2%)
    ppermute x4, waiting for transfers between devices, swapped(): return lax.ppermute(value, axis, pairs)  207 us
    all_to_all x1, blocking collectives, body(): lax.all_to_all(full_pairs, 'row', split_axis=0, concat_axis=1, tiled=True)  118 us
    all_to_all x1, waiting for transfers between devices, body(): lax.all_to_all(local_pairs, 'row', split_axis=1, concat_axis=0, tiled=True)  70.6 us
    pallas_call x4, Pallas kernels, rotation(): pl.pallas_call(rotation_kernel, out_shape=jax.ShapeDtypeStruct((1, W, W),...  49.1 us
    dot_general x4, matrix products, body(): jnp.einsum('rpa,rpb->pab', full_pairs, full_pairs, precision=lax.Precisio...  25.4 us
    dot_general x4, matrix products, body(): jnp.einsum('rpa,pba->rpb', full_pairs, rotator, precision=lax.Precision.H...  24.8 us
    all_to_all x2, local copies, waits for them, and re-layouts, body(): lax.all_to_all(full_pairs, 'row', split_axis=0, concat_axis=1, tiled=True)  23.9 us
    unnamed x8, local copies, waits for them, and re-layouts  18.6 us
  transfers between devices with their start and end apart: 5, of which 5 were waited for; matrix products, arithmetic and copies ran while one was open for 0% of the time, Pallas kernels for 0%

profile of v1, /device:TPU:0, one launch (start us, length us, event | category | flops | bytes accessed | tf_op | source)
XLA Modules:
  0.0 604.3 jit_solution(6911885336224124573)
XLA Ops:
  2.8 6.6 %copy.14 = f32[1024,1536]{0,1:T(8,128)} copy(f32[1024,1536]{1,0:T(8,128)} %param.3) | data formatting | bytes 12582912 | tf_op args[0]
  9.3 6.4 %gather_fusion = f32[16,1024,96]{1,2,0:T(8,128)} fusion(f32[1024,16,96]{0,2,1:T(8,128)} %bitcast.171, s32[1024]{0:T(1024)S(1)} %pad_clamp_fusion), kind=kCustom, calls=%fused_computation | custom fusion | bytes 12582976 | tf_op jit(solution)/shard_map/jit(_take)/gather | solution.py:121
  15.7 6.0 broadcast_select_fusion
  21.7 5.7 all-to-all-start
  28.8 70.6 %all-to-all-done = f32[1024,8,192]{0,2,1:T(8,128)} async-done(((f32[1024,8,192]{0,2,1:T(8,128)}), f32[1024,8,192]{0,2,1:T(8,128)}, u32[]{:S(2)}, u32[]{:S(2)}) %all-to-all-start) | async-done | bytes 6291488 | tf_op jit(solution)/shard_map/all_to_all | solution.py:123
  99.4 9.8 %fusion.6.gram_ref = f32[1,192,192]{2,1,0:T(8,128)S(1)} fusion(f32[1024,8,192]{0,2,1:T(8,128)} %all-to-all-done), kind=kOutput, calls=%fused_computation.28 | convolution fusion | flops 3623878656 | bytes 6438912 | tf_op jit(solution)/shard_map/rpa,rpb->pab/dot_general | solution.py:126
  109.2 12.2 %rotation.4 = f32[1,192,192]{2,1,0:T(8,128)S(1)} custom-call(f32[1,192,192]{2,1,0:T(8,128)S(1)} %fusion.6.gram_ref), custom_call_target="tpu_custom_call" | custom-call | tf_op jit(solution)/shard_map/rotation/pallas_call | solution.py:91
  124.8 6.2 %fusion.15 = f32[192,8192]{1,0:T(8,128)S(1)} fusion(f32[8192,192]{0,1:T(8,128)S(1)} %bitcast.172, f32[1,192,192]{2,1,0:T(8,128)S(1)} %rotation.4), kind=kOutput, calls=%fused_computation.38 | convolution fusion | flops 3623878656 | bytes 12730368 | tf_op jit(solution)/shard_map/rpa,pba->rpb/dot_general | solution.py:130
  138.7 5.2 convolution_bitcast_fusion.2.gram_ref
  143.9 12.2 %rotation.5 = f32[1,192,192]{2,1,0:T(8,128)S(1)} custom-call(f32[1,192,192]{2,1,0:T(8,128)S(1)} %convolution_bitcast_fusion.2.gram_ref), custom_call_target="tpu_custom_call" | custom-call | tf_op jit(solution)/shard_map/rotation/pallas_call | solution.py:91
  156.1 6.2 %fusion.13 = f32[192,8192]{1,0:T(8,128)S(1)} fusion(f32[8192,192]{0,1:T(8,128)S(1)} %bitcast.157, f32[1,192,192]{2,1,0:T(8,128)S(1)} %rotation.5), kind=kOutput, calls=%fused_computation.36 | convolution fusion | flops 3623878656 | bytes 12730368 | tf_op jit(solution)/shard_map/rpa,pba->rpb/dot_general | solution.py:130
  165.2 67.9 %collective-permute-done.1 = f32[8192,1,96]{0,2,1:T(8,128)S(1)} collective-permute-done((f32[8192,1,96]{0,2,1:T(8,128)S(1)}, f32[8192,1,96]{0,2,1:T(8,128)S(1)}, u32[]{:S(2)}, u32[]{:S(2)}) %collective-permute-start.1) | collective-permute-done | bytes 3145760 | tf_op jit(solution)/shard_map/ppermute | solution.py:16
  239.5 12.4 %rotation.6 = f32[1,192,192]{2,1,0:T(8,128)S(1)} custom-call(f32[1,192,192]{2,1,0:T(8,128)S(1)} %convolution_bitcast_fusion.1.gram_ref), custom_call_target="tpu_custom_call" | custom-call | tf_op jit(solution)/shard_map/rotation/pallas_call | solution.py:91
  251.9 6.2 %fusion.11 = f32[192,8192]{1,0:T(8,128)S(1)} fusion(f32[8192,192]{0,1:T(8,128)S(1)} %bitcast.159, f32[1,192,192]{2,1,0:T(8,128)S(1)} %rotation.6), kind=kOutput, calls=%fused_computation.34 | convolution fusion | flops 3623878656 | bytes 12730368 | tf_op jit(solution)/shard_map/rpa,pba->rpb/dot_general | solution.py:130
  262.5 67.0 %collective-permute-done.2 = f32[8192,1,96]{0,2,1:T(8,128)S(1)} collective-permute-done((f32[8192,1,96]{0,2,1:T(8,128)S(1)}, f32[8192,1,96]{0,2,1:T(8,128)S(1)}, u32[]{:S(2)}, u32[]{:S(2)}) %collective-permute-start.2) | collective-permute-done | bytes 3145760 | tf_op jit(solution)/shard_map/ppermute | solution.py:16
  335.9 12.2 %rotation.7 = f32[1,192,192]{2,1,0:T(8,128)S(1)} custom-call(f32[1,192,192]{2,1,0:T(8,128)S(1)} %convolution_bitcast_fusion.gram_ref), custom_call_target="tpu_custom_call" | custom-call | tf_op jit(solution)/shard_map/rotation/pallas_call | solution.py:91
  348.1 6.2 %fusion.9 = f32[192,8192]{1,0:T(8,128)S(1)} fusion(f32[8192,192]{0,1:T(8,128)S(1)} %bitcast.161, f32[1,192,192]{2,1,0:T(8,128)S(1)} %rotation.7), kind=kOutput, calls=%fused_computation.32 | convolution fusion | flops 3623878656 | bytes 12730368 | tf_op jit(solution)/shard_map/rpa,pba->rpb/dot_general | solution.py:130
  358.3 66.6 %collective-permute-done.3 = f32[8192,1,96]{0,2,1:T(8,128)S(1)} collective-permute-done((f32[8192,1,96]{0,2,1:T(8,128)S(1)}, f32[8192,1,96]{0,2,1:T(8,128)S(1)}, u32[]{:S(2)}, u32[]{:S(2)}) %collective-permute-start.3) | collective-permute-done | bytes 3145760 | tf_op jit(solution)/shard_map/ppermute | solution.py:16
  428.9 18.0 %copy.16 = f32[8192,1,192]{2,1,0:T(1,128)} copy(f32[8192,1,192]{0,2,1:T(8,128)} %bitcast.173) | data formatting | bytes 12582912 | tf_op jit(solution)/shard_map/reshape | solution.py:112
  446.9 118.3 %all_to_all.30 = f32[8192,1,192]{2,1,0:T(1,128)} all-to-all(f32[8192,1,192]{2,1,0:T(1,128)} %copy.16), channel_id=1, replica_groups=mesh['row'=8,'col'=16] {'row'}, dimensions={0} | all-to-all | bytes 12582912 | tf_op jit(solution)/shard_map/all_to_all | solution.py:134
  565.2 17.6 %copy.17 = f32[8192,1,192]{0,2,1:T(8,128)} copy(f32[8192,1,192]{2,1,0:T(1,128)} %all_to_all.30) | data formatting | bytes 12582912 | tf_op jit(solution)/shard_map/all_to_all | solution.py:134
  582.8 8.2 %copy.21 = f32[24,8,8,1024]{3,2,1,0:T(8,128)S(1)} copy(f32[24,8,8,1024]{3,1,2,0:T(8,128)} %bitcast.174) | data formatting | bytes 12582912
  591.0 6.3 %copy.18 = f32[1024,8,1,192]{0,3,1,2:T(8,128)} copy(f32[1024,8,1,192]{0,1,3,2:T(8,128)S(1)} %bitcast.175) | data formatting | bytes 12582912 | tf_op jit(solution)/shard_map/all_to_all | solution.py:134
  597.3 6.6 %copy.19 = f32[1024,1536]{1,0:T(8,128)} copy(f32[1024,1536]{0,1:T(8,128)} %bitcast.176) | data formatting | bytes 12582912 | tf_op jit(solution)/shard_map/reshape | solution.py:135
  (34 shorter events, 40.3 us)
Async XLA Ops:
  0.0 27.5 %copy-start = (s32[4,8]{1,0:T(4,128)S(1)}, s32[4,8]{1,0:T(4,128)}, u32[]{:S(2)}) copy-start(s32[4,8]{1,0:T(4,128)} %param.5) | copy-start | bytes 388
  21.7 77.7 %all-to-all-start = ((f32[1024,8,192]{0,2,1:T(8,128)}), f32[1024,8,192]{0,2,1:T(8,128)}, u32[]{:S(2)}, u32[]{:S(2)}) async-start(f32[1024,8,192]{0,2,1:T(8,128)} %broadcast_select_fusion), calls=%async_computation | async-start | bytes 12582912 | tf_op jit(solution)/shard_map/all_to_all | solution.py:123
  131.4 6.1 %collective-permute-start = (f32[8192,1,96]{0,2,1:T(8,128)S(1)}, f32[8192,1,96]{0,2,1:T(8,128)S(1)}, u32[]{:S(2)}, u32[]{:S(2)}) collective-permute-start(f32[8192,1,96]{0,2,1:T(8,128)S(1)} %fusion.2), channel_id=1, source_target_pairs={{0,1},{1,0},{2,3},{3,2},{4,5},{5,4},{6,7},{7,6},{8,9},{9,8},{10,11... | collective-permute-start | bytes 9437192 | tf_op jit(solution)/shard_map/ppermute | solution.py:16
  162.7 70.4 %collective-permute-start.1 = (f32[8192,1,96]{0,2,1:T(8,128)S(1)}, f32[8192,1,96]{0,2,1:T(8,128)S(1)}, u32[]{:S(2)}, u32[]{:S(2)}) collective-permute-start(f32[8192,1,96]{0,2,1:T(8,128)S(1)} %fusion.3), channel_id=1, source_target_pairs={{0,2},{1,3},{2,0},{3,1},{4,6},{5,7},{6,4},{7,5},{8,10},{9,11},{10,... | collective-permute-start | bytes 9437192 | tf_op jit(solution)/shard_map/ppermute | solution.py:16
  258.5 71.1 %collective-permute-start.2 = (f32[8192,1,96]{0,2,1:T(8,128)S(1)}, f32[8192,1,96]{0,2,1:T(8,128)S(1)}, u32[]{:S(2)}, u32[]{:S(2)}) collective-permute-start(f32[8192,1,96]{0,2,1:T(8,128)S(1)} %fusion.4), channel_id=1, source_target_pairs={{0,4},{1,5},{2,6},{3,7},{4,0},{5,1},{6,2},{7,3},{8,12},{9,13},{10,... | collective-permute-start | bytes 9437192 | tf_op jit(solution)/shard_map/ppermute | solution.py:16
  354.7 70.3 %collective-permute-start.3 = (f32[8192,1,96]{0,2,1:T(8,128)S(1)}, f32[8192,1,96]{0,2,1:T(8,128)S(1)}, u32[]{:S(2)}, u32[]{:S(2)}) collective-permute-start(f32[8192,1,96]{0,2,1:T(8,128)S(1)} %fusion.5), channel_id=1, source_target_pairs={{0,8},{1,9},{2,10},{3,11},{4,12},{5,13},{6,14},{7,15},{8,0},{9,1},... | collective-permute-start | bytes 9437192 | tf_op jit(solution)/shard_map/ppermute | solution.py:16
  597.3 6.6 %copy-start.1 = (s32[4,8]{1,0:T(4,128)S(1)}, s32[4,8]{1,0:T(4,128)}, u32[]{:S(2)}) copy-start(s32[4,8]{1,0:T(4,128)} %param.5) | copy-start | bytes 388

commit v2 on v1

v2 whole, which is shorter than its diff:
```python
import functools

import jax
import jax.numpy as jnp
from jax import lax
from jax.experimental import pallas as pl
from jax.experimental.pallas import tpu as pltpu
from jax.sharding import PartitionSpec as P

MESH = pl.DeviceIdType.MESH
BW = 96
F32=jnp.float32; BF=jnp.bfloat16
W=192
def pieces(x):
    h=x.astype(BF); r=x-h.astype(F32); m=r.astype(BF); l=(r-m.astype(F32)).astype(BF)
    return h,m,l
def outer(left, right):
    a0,a1,a2=pieces(left); b0,b1,b2=pieces(right)
    a=jnp.concatenate([a2,a0,a1,a1,a0,a0],0)
    b=jnp.concatenate([b0,b2,b1,b0,b1,b0],0)
    return lax.dot_general(a,b,(((0,),(0,)),((),())),preferred_element_type=F32)
def rsqrt(d):
    r=lax.rsqrt(d)
    return r*(1.5-0.5*d*r*r)
def eliminate(rows, base, NB):
    diag=rows[0][:,base:base+NB]
    cols=[jnp.broadcast_to(diag[:,c:c+1],(NB,128)) for c in range(NB)]
    idx=lax.broadcasted_iota(jnp.int32,(NB,128),0)
    rows=[[r[:,i:i+128] for i in range(0,r.shape[1],128)] for r in rows]
    for c in range(NB):
        col=cols[c]
        r=rsqrt(jnp.broadcast_to(col[c:c+1],(NB,128)))
        l=col*r
        lm=jnp.where(idx>c,l,0.0)
        for q in range(c+1,NB):
            cols[q]=cols[q]-lm*jnp.broadcast_to(l[q:q+1],(NB,128))
        for g in rows:
            for i in range(len(g)):
                u=jnp.broadcast_to(g[i][c:c+1],(NB,128))*r
                g[i]=jnp.where(idx==c,u,g[i]-lm*u)
    return [jnp.concatenate(g,1) if len(g)>1 else g[0] for g in rows]
def factor(a_ref, e_ref, NB):
    for t in range(W//NB):
        j=t*NB
        lo=(j//128)*128
        panel=[a_ref[j:j+NB,lo:]]
        if e_ref is not None: panel.append(e_ref[j:j+NB,:])
        out=eliminate(panel,j-lo,NB)
        u=out[0]
        ri=lax.broadcasted_iota(jnp.int32,u.shape,0)+(j-lo)
        ci=lax.broadcasted_iota(jnp.int32,u.shape,1)
        u=jnp.where(ci>=ri,u,0.0)
        a_ref[j:j+NB,lo:]=u
        if lo: a_ref[j:j+NB,:lo]=jnp.zeros((NB,lo),F32)
        if e_ref is not None: e_ref[j:j+NB,:]=out[1]
        rem=W-j-NB
        if rem==0: break
        left=u[:,j+NB-lo:W-lo]
        a_ref[j+NB:W,lo:]=a_ref[j+NB:W,lo:]-outer(left,u)
        if e_ref is not None:
            e_ref[j+NB:W,:]=e_ref[j+NB:W,:]-outer(left,out[1])
def rotate(g, a_ref, e_ref, NB):
    s=jnp.sum(jnp.sum(g*g,axis=0,keepdims=True),axis=1,keepdims=True)
    y=g/jnp.sqrt(s)
    yy=y[:,:W]
    a_ref[:,:W]=lax.dot_general(yy,yy,(((0,),(0,)),((),())),precision=lax.Precision.HIGHEST,preferred_element_type=F32)
    a_ref[:,W:]=jnp.zeros((W,256-W),F32)
    factor(a_ref,None,NB)
    u=a_ref[...]
    e_ref[...]=u
    uu=u[:,:W]
    a_ref[:,:W]=lax.dot_general(uu,uu,(((1,),(1,)),((),())),precision=lax.Precision.HIGHEST,preferred_element_type=F32)
    a_ref[:,W:]=jnp.zeros((W,256-W),F32)
    factor(a_ref,e_ref,NB)
STEPS = 4
ROWS_LOCAL = 1024
VMEM_LIMIT = 60 * 2**20


def split_two(x):
    high = x.astype(BF)
    return high, (x - high.astype(F32)).astype(BF)


def pack_gram(gram, ref):
    ref[0:W, :] = gram[:, 0:128]
    ref[W : W + 64, :] = jnp.concatenate([gram[128:W, 128:W], jnp.zeros((64, 64), F32)], 1)


def unpack_gram(packed):
    right = jnp.concatenate([jnp.transpose(packed[128:W, :]), packed[W : W + 64, 0:64]], 0)
    return jnp.concatenate([packed[0:W, :], right], 1)


def swap_rows(x):
    return jnp.concatenate([x[BW:], x[:BW]], 0)


def swap_columns(x):
    return jnp.concatenate([x[:, BW:], x[:, :BW]], 1)


def pair_kernel(
    pairs, slot_ref, first_ref, second_ref, kept_out, came_out,
    kept, came, leaving, gram_out, gram_in, turn, a_ref, e_ref,
    gram_sent, gram_came, turn_sent, turn_came, block_sent, block_came, local_sem,
):
    row = lax.axis_index("row")
    col = lax.axis_index("col")
    half = pairs // 2

    def partner(step):
        stride = (step * step * step + 5 * step + 6) // 6
        return col + stride * (1 - 2 * ((col // stride) % 2))

    barrier = pltpu.get_barrier_semaphore()
    for shift in range(1, pairs):
        pl.semaphore_signal(barrier, inc=1, device_id=((row + shift) % pairs, col), device_id_type=MESH)
    for step in range(STEPS):
        pl.semaphore_signal(barrier, inc=1, device_id=(row, partner(step)), device_id_type=MESH)

    load_first = pltpu.make_async_copy(first_ref, kept, local_sem.at[0])
    load_second = pltpu.make_async_copy(second_ref, came.at[0], local_sem.at[1])
    load_first.start()
    load_second.start()
    load_first.wait()
    load_second.wait()
    pl.semaphore_wait(barrier, pairs - 1 + STEPS)

    def gram_copy(step, pair):
        return pltpu.make_async_remote_copy(
            src_ref=gram_out.at[pair], dst_ref=gram_in.at[step, row], send_sem=gram_sent.at[pair],
            recv_sem=gram_came.at[step, row], device_id=(pair, col), device_id_type=MESH)

    def gram_arrival(step, source):
        return pltpu.make_async_remote_copy(
            src_ref=gram_out.at[source], dst_ref=gram_in.at[step, source], send_sem=gram_sent.at[source],
            recv_sem=gram_came.at[step, source], device_id=(source, col), device_id_type=MESH)

    def turn_copy(step, target):
        return pltpu.make_async_remote_copy(
            src_ref=turn.at[step, row], dst_ref=turn.at[step, row], send_sem=turn_sent.at[target],
            recv_sem=turn_came.at[step, row], device_id=(target, col), device_id_type=MESH)

    def turn_arrival(step, pair):
        return pltpu.make_async_remote_copy(
            src_ref=turn.at[step, pair], dst_ref=turn.at[step, pair], send_sem=turn_sent.at[pair],
            recv_sem=turn_came.at[step, pair], device_id=(pair, col), device_id_type=MESH)

    def block_copy(step, pair):
        return pltpu.make_async_remote_copy(
            src_ref=leaving.at[pair], dst_ref=came.at[step + 1, pair], send_sem=block_sent.at[pair],
            recv_sem=block_came.at[step, pair], device_id=(row, partner(step)), device_id_type=MESH)

    def load_pair(step, pair):
        return split_two(jnp.concatenate([kept[pair], came[step, pair]], 0))

    def phase(index, _):
        split = jnp.minimum(index // 2, 1)
        step = (1 - split) * index + split * (2 + (index - 2) // 2)
        start = split * half * (index % 2)
        count = pairs - split * half
        mine = (row >= start) & (row < start + count)

        def gram_one(pair, _):
            @pl.when(step > 0)
            def _():
                block_copy(step - 1, pair).wait_recv()

            high, low = load_pair(step, pair)
            gram = lax.dot_general(
                jnp.concatenate([low, high, high], 1), jnp.concatenate([high, low, high], 1),
                (((1,), (1,)), ((), ())), preferred_element_type=F32)

            @pl.when(pair == row)
            def _():
                pack_gram(gram, gram_in.at[step, row])

            @pl.when(pair != row)
            def _():
                pack_gram(gram, gram_out.at[pair])
                gram_copy(step, pair).start()

            return 0

        lax.fori_loop(start, start + count, gram_one, 0)

        @pl.when(mine)
        def _():
            def arrive(shift, _):
                gram_arrival(step, (row + shift) % pairs).wait_recv()
                return 0

            lax.fori_loop(1, pairs, arrive, 0)
            total = gram_in[step, 0]
            for source in range(1, pairs):
                total = total + gram_in[step, source]
            gram = unpack_gram(total)
            came_first = (step > 0) & (slot_ref[jnp.maximum(step - 1, 0), row] == 0)
            gram = jnp.where(came_first, swap_columns(swap_rows(gram)), gram)
            rotate(gram, a_ref, e_ref, 32)
            turned = e_ref[:, :W]
            turned = jnp.where(came_first, swap_columns(turned), turned)
            turned = jnp.where(slot_ref[step, row] == 0, swap_rows(turned), turned)
            own = turn.at[step, row]
            own[0:W, :] = turned[:, 0:128]
            own[W:, :] = jnp.concatenate([turned[0:BW, 128:W], turned[BW:W, 128:W]], 1)

            def send(shift, _):
                turn_copy(step, (row + shift) % pairs).start()
                return 0

            lax.fori_loop(1, pairs, send, 0)

        def update_one(pair, _):
            @pl.when(pair != row)
            def _():
                turn_arrival(step, pair).wait_recv()
                gram_copy(step, pair).wait_send()

            @pl.when(step > 0)
            def _():
                block_copy(step - 1, pair).wait_send()

            packed = turn[step, pair]
            tail = packed[W:, :]
            turned = jnp.concatenate(
                [packed[0:W, :], jnp.concatenate([tail[:, 0:64], tail[:, 64:128]], 0)], 1)
            turn_high, turn_low = split_two(turned)
            high, low = load_pair(step, pair)
            dims = (((1,), (0,)), ((), ()))
            new = (
                lax.dot_general(turn_low, high, dims, preferred_element_type=F32)
                + lax.dot_general(turn_high, low, dims, preferred_element_type=F32)
                + lax.dot_general(turn_high, high, dims, preferred_element_type=F32))
            kept[pair] = new[0:BW]
            leaving[pair] = new[BW:]
            block_copy(step, pair).start()
            return 0

        lax.fori_loop(start, start + count, update_one, 0)

        @pl.when(mine)
        def _():
            def sent(shift, _):
                turn_copy(step, (row + shift) % pairs).wait_send()
                return 0

            lax.fori_loop(1, pairs, sent, 0)

        return 0

    lax.fori_loop(0, 6, phase, 0)

    store_kept = pltpu.make_async_copy(kept, kept_out, local_sem.at[0])
    store_kept.start()

    def finish(pair, _):
        block_copy(STEPS - 1, pair).wait()
        return 0

    lax.fori_loop(0, pairs, finish, 0)
    store_came = pltpu.make_async_copy(came.at[STEPS], came_out, local_sem.at[1])
    store_came.start()
    store_kept.wait()
    store_came.wait()


def pair_steps(send_slot, first, second):
    pairs, width, rows = first.shape
    block = jax.ShapeDtypeStruct(first.shape, F32)
    dma = pltpu.SemaphoreType.DMA
    return pl.pallas_call(
        functools.partial(pair_kernel, pairs),
        out_shape=[block, block],
        in_specs=[
            pl.BlockSpec(memory_space=pltpu.SMEM),
            pl.BlockSpec(memory_space=pl.ANY),
            pl.BlockSpec(memory_space=pl.ANY),
        ],
        out_specs=[pl.BlockSpec(memory_space=pl.ANY)] * 2,
        scratch_shapes=[
            pltpu.VMEM((pairs, width, rows), F32),
            pltpu.VMEM((STEPS + 1, pairs, width, rows), F32),
            pltpu.VMEM((pairs, width, rows), F32),
            pltpu.VMEM((pairs, 256, 128), F32),
            pltpu.VMEM((STEPS, pairs, 256, 128), F32),
            pltpu.VMEM((STEPS, pairs, 288, 128), F32),
            pltpu.VMEM((W, 256), F32),
            pltpu.VMEM((W, 256), F32),
            dma((pairs,)),
            dma((STEPS, pairs)),
            dma((pairs,)),
            dma((STEPS, pairs)),
            dma((pairs,)),
            dma((STEPS, pairs)),
            dma((2,)),
        ],
        compiler_params=pltpu.CompilerParams(
            collective_id=0, has_side_effects=True, vmem_limit_bytes=VMEM_LIMIT),
        name="pair_steps",
    )(send_slot, first, second)


def gather_kernel(order_ref, hessian_ref, first_ref, second_ref, turned):
    chunk = hessian_ref.shape[0]
    for part in range(hessian_ref.shape[1] // 384):
        turned[4 * part : 4 * part + 4] = jnp.transpose(
            hessian_ref[:, 384 * part : 384 * part + 384]).reshape(4, BW, chunk)
    for pair in range(first_ref.shape[0]):
        first_ref[pair] = turned[order_ref[0, 2 * pair]]
        second_ref[pair] = turned[order_ref[0, 2 * pair + 1]]


def gathered(hessian, block_order):
    rows, columns = hessian.shape
    blocks = columns // BW
    chunk = 256
    shape = jax.ShapeDtypeStruct((blocks // 2, BW, rows), F32)
    spec = pl.BlockSpec((blocks // 2, BW, chunk), lambda i: (0, 0, i))
    return pl.pallas_call(
        gather_kernel,
        grid=(rows // chunk,),
        out_shape=[shape, shape],
        in_specs=[
            pl.BlockSpec(memory_space=pltpu.SMEM),
            pl.BlockSpec((chunk, columns), lambda i: (i, 0)),
        ],
        out_specs=[spec, spec],
        scratch_shapes=[pltpu.VMEM((blocks, BW, chunk), F32)],
        compiler_params=pltpu.CompilerParams(vmem_limit_bytes=32 * 2**20),
        name="gathered",
    )(block_order, hessian)


def scatter_kernel(slot_ref, kept_ref, came_ref, out_ref):
    for pair in range(0, kept_ref.shape[0], 2):
        parts = []
        for each in (pair, pair + 1):
            came_first = slot_ref[STEPS - 1, each] == 0
            kept, came = kept_ref[each], came_ref[each]
            parts += [jnp.where(came_first, came, kept), jnp.where(came_first, kept, came)]
        out_ref[:, 192 * pair : 192 * pair + 384] = jnp.transpose(jnp.concatenate(parts, 0))


def scattered(send_slot, kept, came):
    pairs, width, rows = kept.shape
    chunk = 256
    spec = pl.BlockSpec((pairs, width, chunk), lambda i: (0, 0, i))
    return pl.pallas_call(
        scatter_kernel,
        grid=(rows // chunk,),
        out_shape=jax.ShapeDtypeStruct((rows, pairs * 2 * width), F32),
        in_specs=[pl.BlockSpec(memory_space=pltpu.SMEM), spec, spec],
        out_specs=pl.BlockSpec((chunk, pairs * 2 * width), lambda i: (i, 0)),
        compiler_params=pltpu.CompilerParams(vmem_limit_bytes=32 * 2**20),
        name="scattered",
    )(send_slot, kept, came)


def body(hessian, block_order, send_slot):
    first, second = gathered(hessian, block_order)
    kept, came = pair_steps(send_slot, first, second)
    return scattered(send_slot, kept, came)


def solution(mesh):
    in_specs = (P("row", "col"), P("col", None), P(None, "col"))
    out_specs = P("row", "col")
    return jax.shard_map(body, mesh=mesh, in_specs=in_specs, out_specs=out_specs, check_vma=False)
```

time: 616 us -> 377 us (0.61); the launches traced: 604 us -> 372 us
  Pallas kernels: 49.1 us -> 362 us
  waiting for transfers between devices: 277 us -> 0 us
  blocking collectives: 118 us -> 0 us
  local copies, waits for them, and re-layouts: 74.5 us -> 10.5 us
  matrix products: 50.2 us -> 0 us
  other arithmetic: 16.6 us -> 0 us
  starting transfers between devices: 15.2 us -> 0 us
    pallas_call x4 -> x3, Pallas kernels: 49.1 us -> 362 us  [the longest x1 354 us: pair_steps(): pl.pallas_call(functools.partial(pair_kernel, pairs), out_shape=[block, b...]
    ppermute x4 -> x0, waiting for transfers between devices: 207 us -> none  [swapped(): return lax.ppermute(value, axis, pairs)]
    all_to_all x1 -> x0, blocking collectives: 118 us -> none  [body(): lax.all_to_all(full_pairs, 'row', split_axis=0, concat_axis=1, tiled=True)]
    all_to_all x1 -> x0, waiting for transfers between devices: 70.6 us -> none  [body(): lax.all_to_all(local_pairs, 'row', split_axis=1, concat_axis=0, tiled=True)]
    dot_general x8 -> x0, matrix products: 50.2 us -> none  [the longest x4 25.4 us: body(): jnp.einsum('rpa,rpb->pab', full_pairs, full_pairs, precision=lax.Precisio...]
    reshape x2 -> x0, local copies, waits for them, and re-layouts: 24.6 us -> none  [the longest x1 18 us: swap_step(): jnp.stack([slot_zero, slot_one], axis=2)]
    all_to_all x2 -> x0, local copies, waits for them, and re-layouts: 23.9 us -> none  [body(): lax.all_to_all(full_pairs, 'row', split_axis=0, concat_axis=1, tiled=True)]
    ppermute x4 -> x0, starting transfers between devices: 9.47 us -> none  [swapped(): return lax.ppermute(value, axis, pairs)]
  transfers between devices with their start and end apart: 5 -> 0, of which waited for: 5 -> 0; matrix products, arithmetic and copies ran while one was open for 0% -> 0% of each run, Pallas kernels for 0% -> 0%
where the time goes in v2:
time: 377 us; the launch traced here: 372 us
  Pallas kernels  362 us (96%)
  local copies, waits for them, and re-layouts  10.5 us (3%)
    pallas_call x1, Pallas kernels, pair_steps(): pl.pallas_call(functools.partial(pair_kernel, pairs), out_shape=[block, b...  354 us
    unnamed x14, local copies, waits for them, and re-layouts  10.5 us

profile of v2, /device:TPU:0, one launch (start us, length us, event | category | flops | bytes accessed | tf_op | source)
XLA Modules:
  0.0 372.3 jit_solution(2002993826134458561)
XLA Ops:
  0.0 0.0 copy-start
  0.0 2.8 copy-done
  2.8 0.0 copy-start.6
  2.8 0.7 copy-done.6
  3.4 3.4 gathered.1
  6.8 0.0 copy-start.1
  6.9 1.7 copy-done.1
  8.5 0.0 copy-start.2
  8.5 1.6 copy-done.2
  10.2 0.0 copy-start.5
  10.2 353.7 %pair_steps.1 = (f32[8,96,1024]{2,1,0:T(8,128)}, f32[8,96,1024]{2,1,0:T(8,128)}) custom-call(s32[4,8]{1,0:T(4,128)} %slot_ref.3, f32[8,96,1024]{2,1,0:T(8,128)} %copy-done.1, f32[8,96,1024]{2,1,0:T(8,128)} %copy-done.2), custom_call_target="tpu_custom_call" | custom-call | tf_op jit(solution)/shard_map/pair_steps/pallas_call | solution.py:273
  363.9 0.0 copy-done.5
  363.9 0.0 copy-start.3
  363.9 1.9 copy-done.3
  365.8 0.0 copy-start.4
  365.8 1.9 copy-done.4
  367.7 4.6 %scattered.1 = f32[1024,1536]{1,0:T(8,128)} custom-call(s32[4,8]{1,0:T(4,128)S(1)} %copy-done.5, f32[8,96,1024]{2,1,0:T(8,128)S(1)} %copy-done.3, f32[8,96,1024]{2,1,0:T(8,128)S(1)} %copy-done.4), custom_call_target="tpu_custom_call" | custom-call | tf_op jit(solution)/shard_map/scattered/pallas_call | solution.py:350
Async XLA Ops:
  0.0 2.8 copy-start
  2.8 0.7 copy-start.6
  6.8 1.7 copy-start.1
  8.5 1.6 copy-start.2
  10.2 353.7 %copy-start.5 = (s32[4,8]{1,0:T(4,128)S(1)}, s32[4,8]{1,0:T(4,128)}, u32[]{:S(2)}) copy-start(s32[4,8]{1,0:T(4,128)} %slot_ref.3) | copy-start | bytes 388
  363.9 1.9 copy-start.3
  365.8 1.9 copy-start.4

commit v3 on v2

--- a/solution.py
+++ b/solution.py
@@ -108,6 +108,10 @@
     row = lax.axis_index("row")
     col = lax.axis_index("col")
     half = pairs // 2
+    own = row // 2 + half * (row % 2)
+
+    def owner(pair):
+        return 2 * (pair % half) + pair // half
 
     def partner(step):
         stride = (step * step * step + 5 * step + 6) // 6
@@ -130,7 +134,7 @@
     def gram_copy(step, pair):
         return pltpu.make_async_remote_copy(
             src_ref=gram_out.at[pair], dst_ref=gram_in.at[step, row], send_sem=gram_sent.at[pair],
-            recv_sem=gram_came.at[step, row], device_id=(pair, col), device_id_type=MESH)
+            recv_sem=gram_came.at[step, row], device_id=(owner(pair), col), device_id_type=MESH)
 
     def gram_arrival(step, source):
         return pltpu.make_async_remote_copy(
@@ -139,13 +143,13 @@
 
     def turn_copy(step, target):
         return pltpu.make_async_remote_copy(
-            src_ref=turn.at[step, row], dst_ref=turn.at[step, row], send_sem=turn_sent.at[target],
-            recv_sem=turn_came.at[step, row], device_id=(target, col), device_id_type=MESH)
+            src_ref=turn.at[step, own], dst_ref=turn.at[step, own], send_sem=turn_sent.at[target],
+            recv_sem=turn_came.at[step, own], device_id=(target, col), device_id_type=MESH)
 
     def turn_arrival(step, pair):
         return pltpu.make_async_remote_copy(
             src_ref=turn.at[step, pair], dst_ref=turn.at[step, pair], send_sem=turn_sent.at[pair],
-            recv_sem=turn_came.at[step, pair], device_id=(pair, col), device_id_type=MESH)
+            recv_sem=turn_came.at[step, pair], device_id=(owner(pair), col), device_id_type=MESH)
 
     def block_copy(step, pair):
         return pltpu.make_async_remote_copy(
@@ -160,7 +164,7 @@
         step = (1 - split) * index + split * (2 + (index - 2) // 2)
         start = split * half * (index % 2)
         count = pairs - split * half
-        mine = (row >= start) & (row < start + count)
+        mine = (own >= start) & (own < start + count)
 
         def gram_one(pair, _):
             @pl.when(step > 0)
@@ -172,11 +176,11 @@
                 jnp.concatenate([low, high, high], 1), jnp.concatenate([high, low, high], 1),
                 (((1,), (1,)), ((), ())), preferred_element_type=F32)
 
-            @pl.when(pair == row)
+            @pl.when(pair == own)
             def _():
                 pack_gram(gram, gram_in.at[step, row])
 
-            @pl.when(pair != row)
+            @pl.when(pair != own)
             def _():
                 pack_gram(gram, gram_out.at[pair])
                 gram_copy(step, pair).start()
@@ -196,15 +200,15 @@
             for source in range(1, pairs):
                 total = total + gram_in[step, source]
             gram = unpack_gram(total)
-            came_first = (step > 0) & (slot_ref[jnp.maximum(step - 1, 0), row] == 0)
+            came_first = (step > 0) & (slot_ref[jnp.maximum(step - 1, 0), own] == 0)
             gram = jnp.where(came_first, swap_columns(swap_rows(gram)), gram)
             rotate(gram, a_ref, e_ref, 32)
             turned = e_ref[:, :W]
             turned = jnp.where(came_first, swap_columns(turned), turned)
-            turned = jnp.where(slot_ref[step, row] == 0, swap_rows(turned), turned)
-            own = turn.at[step, row]
-            own[0:W, :] = turned[:, 0:128]
-            own[W:, :] = jnp.concatenate([turned[0:BW, 128:W], turned[BW:W, 128:W]], 1)
+            turned = jnp.where(slot_ref[step, own] == 0, swap_rows(turned), turned)
+            packed = turn.at[step, own]
+            packed[0:W, :] = turned[:, 0:128]
+            packed[W:, :] = jnp.concatenate([turned[0:BW, 128:W], turned[BW:W, 128:W]], 1)
 
             def send(shift, _):
                 turn_copy(step, (row + shift) % pairs).start()
@@ -213,7 +217,7 @@
             lax.fori_loop(1, pairs, send, 0)
 
         def update_one(pair, _):
-            @pl.when(pair != row)
+            @pl.when(pair != own)
             def _():
                 turn_arrival(step, pair).wait_recv()
                 gram_copy(step, pair).wait_send()
@@ -328,7 +332,7 @@
         ],
         out_specs=[spec, spec],
         scratch_shapes=[pltpu.VMEM((blocks, BW, chunk), F32)],
-        compiler_params=pltpu.CompilerParams(vmem_limit_bytes=32 * 2**20),
+        compiler_params=pltpu.CompilerParams(vmem_limit_bytes=VMEM_LIMIT),
         name="gathered",
     )(block_order, hessian)
 
@@ -353,7 +357,7 @@
         out_shape=jax.ShapeDtypeStruct((rows, pairs * 2 * width), F32),
         in_specs=[pl.BlockSpec(memory_space=pltpu.SMEM), spec, spec],
         out_specs=pl.BlockSpec((chunk, pairs * 2 * width), lambda i: (i, 0)),
-        compiler_params=pltpu.CompilerParams(vmem_limit_bytes=32 * 2**20),
+        compiler_params=pltpu.CompilerParams(vmem_limit_bytes=VMEM_LIMIT),
         name="scattered",
     )(send_slot, kept, came)
 

time: 377 us -> 330 us (0.88); the launches traced: 372 us -> 330 us
  Pallas kernels: 362 us -> 330 us
  local copies, waits for them, and re-layouts: 10.5 us -> 0 us
    pallas_call x1, Pallas kernels: 354 us -> 317 us  [pair_steps(): pl.pallas_call(functools.partial(pair_kernel, pairs), out_shape=[block, b...]
    unnamed x14 -> x0, local copies, waits for them, and re-layouts: 10.5 us -> none
where the time goes in v3:
time: 330 us
  Pallas kernels  330 us (100%)
    pallas_call x1, Pallas kernels, pair_steps(): pl.pallas_call(functools.partial(pair_kernel, pairs), out_shape=[block, b...  317 us
    pallas_call x1, Pallas kernels, gathered(): pl.pallas_call(gather_kernel, grid=(rows // chunk,), out_shape=[shape, sh...  6.82 us

profile of v3, /device:TPU:0, one launch (start us, length us, event | category | flops | bytes accessed | tf_op | source)
XLA Modules:
  0.0 330.0 jit_solution(18135962581370998711)
XLA Ops:
  0.0 6.8 %gathered.1 = (f32[8,96,1024]{2,1,0:T(8,128)}, f32[8,96,1024]{2,1,0:T(8,128)}) custom-call(s32[1,16]{1,0:T(1,128)} %order_ref.1, f32[1024,1536]{1,0:T(8,128)} %hessian_ref.1), custom_call_target="tpu_custom_call" | custom-call | tf_op jit(solution)/shard_map/gathered/pallas_call | solution.py:325
  6.8 316.6 %pair_steps.1 = (f32[8,96,1024]{2,1,0:T(8,128)}, f32[8,96,1024]{2,1,0:T(8,128)}) custom-call(s32[4,8]{1,0:T(4,128)} %slot_ref.3, f32[8,96,1024]{2,1,0:T(8,128)} %get-tuple-element.9.first_ref, f32[8,96,1024]{2,1,0:T(8,128)} %get-tuple-element.10.second_ref), custom_call_target="tpu_custom_call" | custom-call | tf_op jit(solution)/shard_map/pair_steps/pallas_call | solution.py:277
  323.4 6.6 %scattered.1 = f32[1024,1536]{1,0:T(8,128)} custom-call(s32[4,8]{1,0:T(4,128)} %slot_ref.3, f32[8,96,1024]{2,1,0:T(8,128)} %get-tuple-element.11.kept_ref, f32[8,96,1024]{2,1,0:T(8,128)} %get-tuple-element.12.came_ref), custom_call_target="tpu_custom_call" | custom-call | tf_op jit(solution)/shard_map/scattered/pallas_call | solution.py:354

commit v4 on v3

--- a/solution.py
+++ b/solution.py
@@ -22,24 +22,28 @@
 def rsqrt(d):
     r=lax.rsqrt(d)
     return r*(1.5-0.5*d*r*r)
+def recip(d):
+    r = pl.reciprocal(d, approx=True)
+    return r * (2.0 - d * r)
 def eliminate(rows, base, NB):
     diag=rows[0][:,base:base+NB]
     cols=[jnp.broadcast_to(diag[:,c:c+1],(NB,128)) for c in range(NB)]
     idx=lax.broadcasted_iota(jnp.int32,(NB,128),0)
     rows=[[r[:,i:i+128] for i in range(0,r.shape[1],128)] for r in rows]
+    scale=jnp.zeros((NB,128),F32)
     for c in range(NB):
         col=cols[c]
-        r=rsqrt(jnp.broadcast_to(col[c:c+1],(NB,128)))
-        l=col*r
-        lm=jnp.where(idx>c,l,0.0)
+        d=jnp.broadcast_to(col[c:c+1],(NB,128))
+        m=jnp.where(idx>c,col*recip(d),0.0)
+        scale=jnp.where(idx==c,d,scale)
         for q in range(c+1,NB):
-            cols[q]=cols[q]-lm*jnp.broadcast_to(l[q:q+1],(NB,128))
+            cols[q]=cols[q]-m*jnp.broadcast_to(col[q:q+1],(NB,128))
         for g in rows:
             for i in range(len(g)):
-                u=jnp.broadcast_to(g[i][c:c+1],(NB,128))*r
-                g[i]=jnp.where(idx==c,u,g[i]-lm*u)
-    return [jnp.concatenate(g,1) if len(g)>1 else g[0] for g in rows]
-def factor(a_ref, e_ref, NB):
+                g[i]=g[i]-m*jnp.broadcast_to(g[i][c:c+1],(NB,128))
+    scale=rsqrt(scale)
+    return [jnp.concatenate([x*scale for x in g],1) if len(g)>1 else g[0]*scale for g in rows]
+def factor(a_ref, e_ref, NB, ready=None):
     for t in range(W//NB):
         j=t*NB
         lo=(j//128)*128
@@ -53,13 +57,14 @@
         a_ref[j:j+NB,lo:]=u
         if lo: a_ref[j:j+NB,:lo]=jnp.zeros((NB,lo),F32)
         if e_ref is not None: e_ref[j:j+NB,:]=out[1]
+        if ready is not None and (j+NB)%BW==0: ready((j+NB)//BW-1)
         rem=W-j-NB
         if rem==0: break
         left=u[:,j+NB-lo:W-lo]
         a_ref[j+NB:W,lo:]=a_ref[j+NB:W,lo:]-outer(left,u)
         if e_ref is not None:
             e_ref[j+NB:W,:]=e_ref[j+NB:W,:]-outer(left,out[1])
-def rotate(g, a_ref, e_ref, NB):
+def rotate(g, a_ref, e_ref, NB, ready):
     s=jnp.sum(jnp.sum(g*g,axis=0,keepdims=True),axis=1,keepdims=True)
     y=g/jnp.sqrt(s)
     yy=y[:,:W]
@@ -71,7 +76,7 @@
     uu=u[:,:W]
     a_ref[:,:W]=lax.dot_general(uu,uu,(((1,),(1,)),((),())),precision=lax.Precision.HIGHEST,preferred_element_type=F32)
     a_ref[:,W:]=jnp.zeros((W,256-W),F32)
-    factor(a_ref,e_ref,NB)
+    factor(a_ref,e_ref,NB,ready)
 STEPS = 4
 ROWS_LOCAL = 1024
 VMEM_LIMIT = 60 * 2**20
@@ -100,10 +105,23 @@
     return jnp.concatenate([x[:, BW:], x[:, :BW]], 1)
 
 
+def pack_half(half, ref):
+    ref[0:BW, :] = half[:, 0:128]
+    ref[BW:, :] = jnp.concatenate([half[0:48, 128:W], half[48:BW, 128:W]], 1)
+
+
+def unpack_half(packed):
+    tail = packed[BW:, :]
+    right = jnp.concatenate([tail[:, 0:64], tail[:, 64:128]], 0)
+    return jnp.concatenate([packed[0:BW, :], right], 1)
+
+
 def pair_kernel(
     pairs, slot_ref, first_ref, second_ref, kept_out, came_out,
-    kept, came, leaving, gram_out, gram_in, turn, a_ref, e_ref,
-    gram_sent, gram_came, turn_sent, turn_came, block_sent, block_came, local_sem,
+    kept, came, leaving, gram_out, gram_in, cross_out, cross_in, diag_out, diag_in, diag_kept, turn,
+    g_ref, a_ref, e_ref,
+    gram_sent, gram_came, cross_sent, cross_came, diag_sent, diag_came, turn_sent, turn_came,
+    block_sent, block_came, local_sem,
 ):
     row = lax.axis_index("row")
     col = lax.axis_index("col")
@@ -131,33 +149,164 @@
     load_second.wait()
     pl.semaphore_wait(barrier, pairs - 1 + STEPS)
 
-    def gram_copy(step, pair):
-        return pltpu.make_async_remote_copy(
-            src_ref=gram_out.at[pair], dst_ref=gram_in.at[step, row], send_sem=gram_sent.at[pair],
-            recv_sem=gram_came.at[step, row], device_id=(owner(pair), col), device_id_type=MESH)
-
-    def gram_arrival(step, source):
-        return pltpu.make_async_remote_copy(
-            src_ref=gram_out.at[source], dst_ref=gram_in.at[step, source], send_sem=gram_sent.at[source],
-            recv_sem=gram_came.at[step, source], device_id=(source, col), device_id_type=MESH)
-
-    def turn_copy(step, target):
-        return pltpu.make_async_remote_copy(
-            src_ref=turn.at[step, own], dst_ref=turn.at[step, own], send_sem=turn_sent.at[target],
-            recv_sem=turn_came.at[step, own], device_id=(target, col), device_id_type=MESH)
-
-    def turn_arrival(step, pair):
-        return pltpu.make_async_remote_copy(
-            src_ref=turn.at[step, pair], dst_ref=turn.at[step, pair], send_sem=turn_sent.at[pair],
-            recv_sem=turn_came.at[step, pair], device_id=(owner(pair), col), device_id_type=MESH)
+    def gram_copy(pair):
+        return pltpu.make_async_remote_copy(
+            src_ref=gram_out.at[pair], dst_ref=gram_in.at[row], send_sem=gram_sent.at[pair],
+            recv_sem=gram_came.at[row], device_id=(owner(pair), col), device_id_type=MESH)
+
+    def gram_arrival(source):
+        return pltpu.make_async_remote_copy(
+            src_ref=gram_out.at[source], dst_ref=gram_in.at[source], send_sem=gram_sent.at[source],
+            recv_sem=gram_came.at[source], device_id=(source, col), device_id_type=MESH)
+
+    def cross_copy(step, pair):
+        return pltpu.make_async_remote_copy(
+            src_ref=cross_out.at[pair], dst_ref=cross_in.at[step, row], send_sem=cross_sent.at[pair],
+            recv_sem=cross_came.at[step, row], device_id=(owner(pair), col), device_id_type=MESH)
+
+    def cross_arrival(step, source):
+        return pltpu.make_async_remote_copy(
+            src_ref=cross_out.at[source], dst_ref=cross_in.at[step, source], send_sem=cross_sent.at[source],
+            recv_sem=cross_came.at[step, source], device_id=(source, col), device_id_type=MESH)
+
+    def diag_copy(step):
+        return pltpu.make_async_remote_copy(
+            src_ref=diag_out.at[step], dst_ref=diag_in.at[step], send_sem=diag_sent.at[step],
+            recv_sem=diag_came.at[step], device_id=(row, partner(step)), device_id_type=MESH)
+
+    def turn_copy(step, part, target):
+        return pltpu.make_async_remote_copy(
+            src_ref=turn.at[step, own, part], dst_ref=turn.at[step, own, part],
+            send_sem=turn_sent.at[part, target], recv_sem=turn_came.at[step, own, part],
+            device_id=(target, col), device_id_type=MESH)
+
+    def turn_arrival(step, part, pair):
+        return pltpu.make_async_remote_copy(
+            src_ref=turn.at[step, pair, part], dst_ref=turn.at[step, pair, part],
+            send_sem=turn_sent.at[part, pair], recv_sem=turn_came.at[step, pair, part],
+            device_id=(owner(pair), col), device_id_type=MESH)
 
     def block_copy(step, pair):
         return pltpu.make_async_remote_copy(
             src_ref=leaving.at[pair], dst_ref=came.at[step + 1, pair], send_sem=block_sent.at[pair],
             recv_sem=block_came.at[step, pair], device_id=(row, partner(step)), device_id_type=MESH)
 
-    def load_pair(step, pair):
-        return split_two(jnp.concatenate([kept[pair], came[step, pair]], 0))
+    def others(function):
+        def one(shift, _):
+            function((row + shift) % pairs)
+            return 0
+
+        lax.fori_loop(1, pairs, one, 0)
+
+    def gram_full(pair):
+        high, low = split_two(jnp.concatenate([kept[pair], came[0, pair]], 0))
+        gram = lax.dot_general(
+            jnp.concatenate([low, high, high], 1), jnp.concatenate([high, low, high], 1),
+            (((1,), (1,)), ((), ())), preferred_element_type=F32)
+
+        @pl.when(pair == own)
+        def _():
+            pack_gram(gram, gram_in.at[row])
+
+        @pl.when(pair != own)
+        def _():
+            pack_gram(gram, gram_out.at[pair])
+            gram_copy(pair).start()
+
+    def gram_cross(step, pair):
+        block_copy(step - 1, pair).wait_recv()
+        high, low = split_two(kept[pair])
+        came_high, came_low = split_two(came[step, pair])
+        cross = lax.dot_general(
+            jnp.concatenate([low, high, high], 1), jnp.concatenate([came_high, came_low, came_high], 1),
+            (((1,), (1,)), ((), ())), preferred_element_type=F32)
+        cross = jnp.concatenate([cross, jnp.zeros((BW, 128 - BW), F32)], 1)
+
+        @pl.when(pair == own)
+        def _():
+            cross_in[step, row] = cross
+
+        @pl.when(pair != own)
+        def _():
+            cross_out[pair] = cross
+            cross_copy(step, pair).start()
+
+    def gram_whole():
+        others(lambda source: gram_arrival(source).wait_recv())
+        total = gram_in[0]
+        for source in range(1, pairs):
+            total = total + gram_in[source]
+        g_ref[:, :W] = unpack_gram(total)
+
+    def gram_joined(step):
+        others(lambda source: cross_arrival(step, source).wait_recv())
+        diag_copy(step - 1).wait_recv()
+        total = cross_in[step, 0]
+        for source in range(1, pairs):
+            total = total + cross_in[step, source]
+        cross = total[:, :BW]
+        g_ref[0:BW, :W] = jnp.concatenate([diag_kept[:, :BW], cross], 1)
+        g_ref[BW:W, :W] = jnp.concatenate([jnp.transpose(cross), diag_in[step - 1][:, :BW]], 1)
+
+    def own_rotation(step):
+        came_first = (step > 0) & (slot_ref[jnp.maximum(step - 1, 0), own] == 0)
+        gram = g_ref[:, :W]
+        gram = jnp.where(came_first, swap_columns(swap_rows(gram)), gram)
+
+        def ready(part):
+            turned = e_ref[BW * part : BW * part + BW, :W]
+            high, low = split_two(jnp.where(came_first, swap_columns(turned), turned))
+            pack_half(high.astype(F32) + low.astype(F32), turn.at[step, own, part])
+            others(lambda target: turn_copy(step, part, target).start())
+
+        rotate(gram, a_ref, e_ref, 32, ready)
+
+    def turned_of(step, pair):
+        halves = [unpack_half(turn[step, pair, part]) for part in range(2)]
+        sent_first = slot_ref[step, pair] == 0
+        return jnp.concatenate(
+            [jnp.where(sent_first, halves[1], halves[0]), jnp.where(sent_first, halves[0], halves[1])], 0)
+
+    def own_diagonals(step):
+        turned = turned_of(step, own)
+        exact = dict(precision=lax.Precision.HIGHEST, preferred_element_type=F32)
+        product = lax.dot_general(turned, g_ref[:, :W], (((1,), (0,)), ((), ())), **exact)
+        blank = jnp.zeros((BW, 128 - BW), F32)
+        nt = (((1,), (1,)), ((), ()))
+        stays = lax.dot_general(product[:BW], turned[:BW], nt, **exact)
+        leaves = lax.dot_general(product[BW:], turned[BW:], nt, **exact)
+        diag_kept[...] = jnp.concatenate([stays, blank], 1)
+        diag_out[step] = jnp.concatenate([leaves, blank], 1)
+        diag_copy(step).start()
+
+    def update_one(step, pair):
+        @pl.when(pair != own)
+        def _():
+            turn_arrival(step, 0, pair).wait_recv()
+            turn_arrival(step, 1, pair).wait_recv()
+
+            @pl.when(step == 0)
+            def _():
+                gram_copy(pair).wait_send()
+
+            @pl.when(step > 0)
+            def _():
+                cross_copy(step, pair).wait_send()
+
+        @pl.when(step > 0)
+        def _():
+            block_copy(step - 1, pair).wait_send()
+
+        turn_high, turn_low = split_two(turned_of(step, pair))
+        high, low = split_two(jnp.concatenate([kept[pair], came[step, pair]], 0))
+        dims = (((1,), (0,)), ((), ()))
+        new = (
+            lax.dot_general(turn_low, high, dims, preferred_element_type=F32)
+            + lax.dot_general(turn_high, low, dims, preferred_element_type=F32)
+            + lax.dot_general(turn_high, high, dims, preferred_element_type=F32))
+        kept[pair] = new[0:BW]
+        leaving[pair] = new[BW:]
+        block_copy(step, pair).start()
 
     def phase(index, _):
         split = jnp.minimum(index // 2, 1)
@@ -166,91 +315,48 @@
         count = pairs - split * half
         mine = (own >= start) & (own < start + count)
 
-        def gram_one(pair, _):
+        def gram_one(i, _):
+            pair = start + (own + i) % count
+
+            @pl.when(step == 0)
+            def _():
+                gram_full(pair)
+
             @pl.when(step > 0)
             def _():
-                block_copy(step - 1, pair).wait_recv()
-
-            high, low = load_pair(step, pair)
-            gram = lax.dot_general(
-                jnp.concatenate([low, high, high], 1), jnp.concatenate([high, low, high], 1),
-                (((1,), (1,)), ((), ())), preferred_element_type=F32)
-
-            @pl.when(pair == own)
-            def _():
-                pack_gram(gram, gram_in.at[step, row])
-
-            @pl.when(pair != own)
-            def _():
-                pack_gram(gram, gram_out.at[pair])
-                gram_copy(step, pair).start()
+                gram_cross(step, pair)
 
             return 0
 
-        lax.fori_loop(start, start + count, gram_one, 0)
+        lax.fori_loop(0, count, gram_one, 0)
 
         @pl.when(mine)
         def _():
-            def arrive(shift, _):
-                gram_arrival(step, (row + shift) % pairs).wait_recv()
-                return 0
-
-            lax.fori_loop(1, pairs, arrive, 0)
-            total = gram_in[step, 0]
-            for source in range(1, pairs):
-                total = total + gram_in[step, source]
-            gram = unpack_gram(total)
-            came_first = (step > 0) & (slot_ref[jnp.maximum(step - 1, 0), own] == 0)
-            gram = jnp.where(came_first, swap_columns(swap_rows(gram)), gram)
-            rotate(gram, a_ref, e_ref, 32)
-            turned = e_ref[:, :W]
-            turned = jnp.where(came_first, swap_columns(turned), turned)
-            turned = jnp.where(slot_ref[step, own] == 0, swap_rows(turned), turned)
-            packed = turn.at[step, own]
-            packed[0:W, :] = turned[:, 0:128]
-            packed[W:, :] = jnp.concatenate([turned[0:BW, 128:W], turned[BW:W, 128:W]], 1)
-
-            def send(shift, _):
-                turn_copy(step, (row + shift) % pairs).start()
-                return 0
-
-            lax.fori_loop(1, pairs, send, 0)
-
-        def update_one(pair, _):
-            @pl.when(pair != own)
-            def _():
-                turn_arrival(step, pair).wait_recv()
-                gram_copy(step, pair).wait_send()
+            @pl.when(step == 0)
+            def _():
+                gram_whole()
 
             @pl.when(step > 0)
             def _():
-                block_copy(step - 1, pair).wait_send()
-
-            packed = turn[step, pair]
-            tail = packed[W:, :]
-            turned = jnp.concatenate(
-                [packed[0:W, :], jnp.concatenate([tail[:, 0:64], tail[:, 64:128]], 0)], 1)
-            turn_high, turn_low = split_two(turned)
-            high, low = load_pair(step, pair)
-            dims = (((1,), (0,)), ((), ()))
-            new = (
-                lax.dot_general(turn_low, high, dims, preferred_element_type=F32)
-                + lax.dot_general(turn_high, low, dims, preferred_element_type=F32)
-                + lax.dot_general(turn_high, high, dims, preferred_element_type=F32))
-            kept[pair] = new[0:BW]
-            leaving[pair] = new[BW:]
-            block_copy(step, pair).start()
+                gram_joined(step)
+
+            own_rotation(step)
+
+        def update_next(i, _):
+            update_one(step, start + (own + i) % count)
             return 0
 
-        lax.fori_loop(start, start + count, update_one, 0)
+        lax.fori_loop(0, count, update_next, 0)
 
         @pl.when(mine)
         def _():
-            def sent(shift, _):
-                turn_copy(step, (row + shift) % pairs).wait_send()
-                return 0
-
-            lax.fori_loop(1, pairs, sent, 0)
+            @pl.when(step < STEPS - 1)
+            def _():
+                own_diagonals(step)
+                diag_copy(step).wait_send()
+
+            for part in range(2):
+                others(lambda target: turn_copy(step, part, target).wait_send())
 
         return 0
 
@@ -288,14 +394,24 @@
             pltpu.VMEM((STEPS + 1, pairs, width, rows), F32),
             pltpu.VMEM((pairs, width, rows), F32),
             pltpu.VMEM((pairs, 256, 128), F32),
-            pltpu.VMEM((STEPS, pairs, 256, 128), F32),
-            pltpu.VMEM((STEPS, pairs, 288, 128), F32),
+            pltpu.VMEM((pairs, 256, 128), F32),
+            pltpu.VMEM((pairs, width, 128), F32),
+            pltpu.VMEM((STEPS, pairs, width, 128), F32),
+            pltpu.VMEM((STEPS, width, 128), F32),
+            pltpu.VMEM((STEPS, width, 128), F32),
+            pltpu.VMEM((width, 128), F32),
+            pltpu.VMEM((STEPS, pairs, 2, 144, 128), F32),
+            pltpu.VMEM((W, 256), F32),
             pltpu.VMEM((W, 256), F32),
             pltpu.VMEM((W, 256), F32),
             dma((pairs,)),
-            dma((STEPS, pairs)),
+            dma((pairs,)),
             dma((pairs,)),
             dma((STEPS, pairs)),
+            dma((STEPS,)),
+            dma((STEPS,)),
+            dma((2, pairs)),
+            dma((STEPS, pairs, 2)),
             dma((pairs,)),
             dma((STEPS, pairs)),
             dma((2,)),

time: 330 us -> 376 us (1.14)
  Pallas kernels: 330 us -> 375 us
    pallas_call x1, Pallas kernels: 317 us -> 361 us  [pair_steps(): pl.pallas_call(functools.partial(pair_kernel, pairs), out_shape=[block, b...]
where the time goes in v4:
time: 376 us; the launch traced here: 375 us
  Pallas kernels  375 us (100%)
    pallas_call x1, Pallas kernels, pair_steps(): pl.pallas_call(functools.partial(pair_kernel, pairs), out_shape=[block, b...  361 us

profile of v4, /device:TPU:0, one launch (start us, length us, event | category | flops | bytes accessed | tf_op | source)
XLA Modules:
  0.0 374.6 jit_solution(6485107380849239653)
XLA Ops:
  0.0 6.8 %gathered.1 = (f32[8,96,1024]{2,1,0:T(8,128)}, f32[8,96,1024]{2,1,0:T(8,128)}) custom-call(s32[1,16]{1,0:T(1,128)} %order_ref.1, f32[1024,1536]{1,0:T(8,128)} %hessian_ref.1), custom_call_target="tpu_custom_call" | custom-call | tf_op jit(solution)/shard_map/gathered/pallas_call | solution.py:441
  6.8 361.1 %pair_steps.1 = (f32[8,96,1024]{2,1,0:T(8,128)}, f32[8,96,1024]{2,1,0:T(8,128)}) custom-call(s32[4,8]{1,0:T(4,128)} %slot_ref.3, f32[8,96,1024]{2,1,0:T(8,128)} %get-tuple-element.9.first_ref, f32[8,96,1024]{2,1,0:T(8,128)} %get-tuple-element.10.second_ref), custom_call_target="tpu_custom_call" | custom-call | tf_op jit(solution)/shard_map/pair_steps/pallas_call | solution.py:383
  368.0 6.6 %scattered.1 = f32[1024,1536]{1,0:T(8,128)} custom-call(s32[4,8]{1,0:T(4,128)} %slot_ref.3, f32[8,96,1024]{2,1,0:T(8,128)} %get-tuple-element.11.kept_ref, f32[8,96,1024]{2,1,0:T(8,128)} %get-tuple-element.12.came_ref), custom_call_target="tpu_custom_call" | custom-call | tf_op jit(solution)/shard_map/scattered/pallas_call | solution.py:470

commit v5 on v4

--- a/solution.py
+++ b/solution.py
@@ -131,6 +131,9 @@
     def owner(pair):
         return 2 * (pair % half) + pair // half
 
+    def ordered(start, i):
+        return start + half * (i // half) + (row // 2 + half - i % half) % half
+
     def partner(step):
         stride = (step * step * step + 5 * step + 6) // 6
         return col + stride * (1 - 2 * ((col // stride) % 2))
@@ -316,7 +319,7 @@
         mine = (own >= start) & (own < start + count)
 
         def gram_one(i, _):
-            pair = start + (own + i) % count
+            pair = ordered(start, i)
 
             @pl.when(step == 0)
             def _():
@@ -343,7 +346,7 @@
             own_rotation(step)
 
         def update_next(i, _):
-            update_one(step, start + (own + i) % count)
+            update_one(step, ordered(start, i))
             return 0
 
         lax.fori_loop(0, count, update_next, 0)

time: 376 us -> 371 us (0.987)
  Pallas kernels: 375 us -> 371 us
    pallas_call x1, Pallas kernels: 361 us -> 357 us  [pair_steps(): pl.pallas_call(functools.partial(pair_kernel, pairs), out_shape=[block, b...]
where the time goes in v5:
time: 371 us
  Pallas kernels  371 us (100%)
    pallas_call x1, Pallas kernels, pair_steps(): pl.pallas_call(functools.partial(pair_kernel, pairs), out_shape=[block, b...  357 us

profile of v5, /device:TPU:0, one launch (start us, length us, event | category | flops | bytes accessed | tf_op | source)
XLA Modules:
  0.0 370.7 jit_solution(3910253509098100646)
XLA Ops:
  0.0 6.8 %gathered.1 = (f32[8,96,1024]{2,1,0:T(8,128)}, f32[8,96,1024]{2,1,0:T(8,128)}) custom-call(s32[1,16]{1,0:T(1,128)} %order_ref.1, f32[1024,1536]{1,0:T(8,128)} %hessian_ref.1), custom_call_target="tpu_custom_call" | custom-call | tf_op jit(solution)/shard_map/gathered/pallas_call | solution.py:444
  6.8 357.3 %pair_steps.1 = (f32[8,96,1024]{2,1,0:T(8,128)}, f32[8,96,1024]{2,1,0:T(8,128)}) custom-call(s32[4,8]{1,0:T(4,128)} %slot_ref.3, f32[8,96,1024]{2,1,0:T(8,128)} %get-tuple-element.9.first_ref, f32[8,96,1024]{2,1,0:T(8,128)} %get-tuple-element.10.second_ref), custom_call_target="tpu_custom_call" | custom-call | tf_op jit(solution)/shard_map/pair_steps/pallas_call | solution.py:386
  364.1 6.6 %scattered.1 = f32[1024,1536]{1,0:T(8,128)} custom-call(s32[4,8]{1,0:T(4,128)} %slot_ref.3, f32[8,96,1024]{2,1,0:T(8,128)} %get-tuple-element.11.kept_ref, f32[8,96,1024]{2,1,0:T(8,128)} %get-tuple-element.12.came_ref), custom_call_target="tpu_custom_call" | custom-call | tf_op jit(solution)/shard_map/scattered/pallas_call | solution.py:473

commit v6 on v5

--- a/solution.py
+++ b/solution.py
@@ -10,7 +10,7 @@
 MESH = pl.DeviceIdType.MESH
 BW = 96
 F32=jnp.float32; BF=jnp.bfloat16
-W=192
+W=192;BW=96
 def pieces(x):
     h=x.astype(BF); r=x-h.astype(F32); m=r.astype(BF); l=(r-m.astype(F32)).astype(BF)
     return h,m,l
@@ -126,7 +126,10 @@
     row = lax.axis_index("row")
     col = lax.axis_index("col")
     half = pairs // 2
+    across = (row + half) % pairs
+    plane = row // half * half
     own = row // 2 + half * (row % 2)
+    beyond = across // 2 + half * (across % 2)
 
     def owner(pair):
         return 2 * (pair % half) + pair // half
@@ -177,17 +180,17 @@
             src_ref=diag_out.at[step], dst_ref=diag_in.at[step], send_sem=diag_sent.at[step],
             recv_sem=diag_came.at[step], device_id=(row, partner(step)), device_id_type=MESH)
 
-    def turn_copy(step, part, target):
-        return pltpu.make_async_remote_copy(
-            src_ref=turn.at[step, own, part], dst_ref=turn.at[step, own, part],
-            send_sem=turn_sent.at[part, target], recv_sem=turn_came.at[step, own, part],
+    def turn_copy(step, part, pair, target):
+        return pltpu.make_async_remote_copy(
+            src_ref=turn.at[step, pair, part], dst_ref=turn.at[step, pair, part],
+            send_sem=turn_sent.at[part, pair // 2 % 2, target], recv_sem=turn_came.at[step, pair, part],
             device_id=(target, col), device_id_type=MESH)
 
     def turn_arrival(step, part, pair):
         return pltpu.make_async_remote_copy(
             src_ref=turn.at[step, pair, part], dst_ref=turn.at[step, pair, part],
-            send_sem=turn_sent.at[part, pair], recv_sem=turn_came.at[step, pair, part],
-            device_id=(owner(pair), col), device_id_type=MESH)
+            send_sem=turn_sent.at[part, 0, 0], recv_sem=turn_came.at[step, pair, part],
+            device_id=(across, col), device_id_type=MESH)
 
     def block_copy(step, pair):
         return pltpu.make_async_remote_copy(
@@ -200,6 +203,13 @@
             return 0
 
         lax.fori_loop(1, pairs, one, 0)
+
+    def neighbours(function):
+        def one(shift, _):
+            function(plane + (row - plane + shift) % half)
+            return 0
+
+        lax.fori_loop(1, half, one, 0)
 
     def gram_full(pair):
         high, low = split_two(jnp.concatenate([kept[pair], came[0, pair]], 0))
@@ -260,7 +270,8 @@
             turned = e_ref[BW * part : BW * part + BW, :W]
             high, low = split_two(jnp.where(came_first, swap_columns(turned), turned))
             pack_half(high.astype(F32) + low.astype(F32), turn.at[step, own, part])
-            others(lambda target: turn_copy(step, part, target).start())
+            turn_copy(step, part, own, across).start()
+            neighbours(lambda target: turn_copy(step, part, own, target).start())
 
         rotate(gram, a_ref, e_ref, 32, ready)
 
@@ -283,11 +294,13 @@
         diag_copy(step).start()
 
     def update_one(step, pair):
-        @pl.when(pair != own)
+        @pl.when((pair != own) & (pair != beyond))
         def _():
             turn_arrival(step, 0, pair).wait_recv()
             turn_arrival(step, 1, pair).wait_recv()
 
+        @pl.when(pair != own)
+        def _():
             @pl.when(step == 0)
             def _():
                 gram_copy(pair).wait_send()
@@ -344,6 +357,9 @@
                 gram_joined(step)
 
             own_rotation(step)
+            for part in range(2):
+                turn_arrival(step, part, beyond).wait_recv()
+                neighbours(lambda target: turn_copy(step, part, beyond, target).start())
 
         def update_next(i, _):
             update_one(step, ordered(start, i))
@@ -359,7 +375,9 @@
                 diag_copy(step).wait_send()
 
             for part in range(2):
-                others(lambda target: turn_copy(step, part, target).wait_send())
+                turn_copy(step, part, own, across).wait_send()
+                neighbours(lambda target: turn_copy(step, part, own, target).wait_send())
+                neighbours(lambda target: turn_copy(step, part, beyond, target).wait_send())
 
         return 0
 
@@ -413,7 +431,7 @@
             dma((STEPS, pairs)),
             dma((STEPS,)),
             dma((STEPS,)),
-            dma((2, pairs)),
+            dma((2, 2, pairs)),
             dma((STEPS, pairs, 2)),
             dma((pairs,)),
             dma((STEPS, pairs)),

time: 371 us -> 375 us (1.011)
  no operation moved by 1% of the time
where the time goes in v6:
time: 375 us; the launch traced here: 374 us
  Pallas kernels  374 us (100%)
    pallas_call x1, Pallas kernels, pair_steps(): pl.pallas_call(functools.partial(pair_kernel, pairs), out_shape=[block, b...  361 us

profile of v6, /device:TPU:0, one launch (start us, length us, event | category | flops | bytes accessed | tf_op | source)
XLA Modules:
  0.0 374.1 jit_solution(998570661233036637)
XLA Ops:
  0.0 6.8 %gathered.1 = (f32[8,96,1024]{2,1,0:T(8,128)}, f32[8,96,1024]{2,1,0:T(8,128)}) custom-call(s32[1,16]{1,0:T(1,128)} %order_ref.1, f32[1024,1536]{1,0:T(8,128)} %hessian_ref.1), custom_call_target="tpu_custom_call" | custom-call | tf_op jit(solution)/shard_map/gathered/pallas_call | solution.py:462
  6.8 360.7 %pair_steps.1 = (f32[8,96,1024]{2,1,0:T(8,128)}, f32[8,96,1024]{2,1,0:T(8,128)}) custom-call(s32[4,8]{1,0:T(4,128)} %slot_ref.3, f32[8,96,1024]{2,1,0:T(8,128)} %get-tuple-element.9.first_ref, f32[8,96,1024]{2,1,0:T(8,128)} %get-tuple-element.10.second_ref), custom_call_target="tpu_custom_call" | custom-call | tf_op jit(solution)/shard_map/pair_steps/pallas_call | solution.py:404
  367.6 6.6 %scattered.1 = f32[1024,1536]{1,0:T(8,128)} custom-call(s32[4,8]{1,0:T(4,128)} %slot_ref.3, f32[8,96,1024]{2,1,0:T(8,128)} %get-tuple-element.11.kept_ref, f32[8,96,1024]{2,1,0:T(8,128)} %get-tuple-element.12.came_ref), custom_call_target="tpu_custom_call" | custom-call | tf_op jit(solution)/shard_map/scattered/pallas_call | solution.py:491

commit v7 on v6

--- a/solution.py
+++ b/solution.py
@@ -357,6 +357,11 @@
                 gram_joined(step)
 
             own_rotation(step)
+
+            @pl.when(step < STEPS - 1)
+            def _():
+                own_diagonals(step)
+
             for part in range(2):
                 turn_arrival(step, part, beyond).wait_recv()
                 neighbours(lambda target: turn_copy(step, part, beyond, target).start())
@@ -371,7 +376,6 @@
         def _():
             @pl.when(step < STEPS - 1)
             def _():
-                own_diagonals(step)
                 diag_copy(step).wait_send()
 
             for part in range(2):

time: 375 us -> 300 us (0.80)
  Pallas kernels: 374 us -> 299 us
    pallas_call x1, Pallas kernels: 361 us -> 285 us  [pair_steps(): pl.pallas_call(functools.partial(pair_kernel, pairs), out_shape=[block, b...]
where the time goes in v7:
time: 300 us; the launch traced here: 299 us
  Pallas kernels  299 us (100%)
    pallas_call x1, Pallas kernels, pair_steps(): pl.pallas_call(functools.partial(pair_kernel, pairs), out_shape=[block, b...  285 us
    pallas_call x1, Pallas kernels, gathered(): pl.pallas_call(gather_kernel, grid=(rows // chunk,), out_shape=[shape, sh...  6.82 us
    pallas_call x1, Pallas kernels, scattered(): pl.pallas_call(scatter_kernel, grid=(rows // chunk,), out_shape=jax.Shape...  6.57 us

profile of v7, /device:TPU:0, one launch (start us, length us, event | category | flops | bytes accessed | tf_op | source)
XLA Modules:
  0.0 298.7 jit_solution(17146659141825783646)
XLA Ops:
  0.0 6.8 %gathered.1 = (f32[8,96,1024]{2,1,0:T(8,128)}, f32[8,96,1024]{2,1,0:T(8,128)}) custom-call(s32[1,16]{1,0:T(1,128)} %order_ref.1, f32[1024,1536]{1,0:T(8,128)} %hessian_ref.1), custom_call_target="tpu_custom_call" | custom-call | tf_op jit(solution)/shard_map/gathered/pallas_call | solution.py:466
  6.8 285.3 %pair_steps.1 = (f32[8,96,1024]{2,1,0:T(8,128)}, f32[8,96,1024]{2,1,0:T(8,128)}) custom-call(s32[4,8]{1,0:T(4,128)} %slot_ref.3, f32[8,96,1024]{2,1,0:T(8,128)} %get-tuple-element.9.first_ref, f32[8,96,1024]{2,1,0:T(8,128)} %get-tuple-element.10.second_ref), custom_call_target="tpu_custom_call" | custom-call | tf_op jit(solution)/shard_map/pair_steps/pallas_call | solution.py:408
  292.1 6.6 %scattered.1 = f32[1024,1536]{1,0:T(8,128)} custom-call(s32[4,8]{1,0:T(4,128)} %slot_ref.3, f32[8,96,1024]{2,1,0:T(8,128)} %get-tuple-element.11.kept_ref, f32[8,96,1024]{2,1,0:T(8,128)} %get-tuple-element.12.came_ref), custom_call_target="tpu_custom_call" | custom-call | tf_op jit(solution)/shard_map/scattered/pallas_call | solution.py:495

commit v8 on v7

--- a/solution.py
+++ b/solution.py
@@ -8,7 +8,7 @@
 from jax.sharding import PartitionSpec as P
 
 MESH = pl.DeviceIdType.MESH
-BW = 96
+
 F32=jnp.float32; BF=jnp.bfloat16
 W=192;BW=96
 def pieces(x):
@@ -23,8 +23,7 @@
     r=lax.rsqrt(d)
     return r*(1.5-0.5*d*r*r)
 def recip(d):
-    r = pl.reciprocal(d, approx=True)
-    return r * (2.0 - d * r)
+    return 1.0/d
 def eliminate(rows, base, NB):
     diag=rows[0][:,base:base+NB]
     cols=[jnp.broadcast_to(diag[:,c:c+1],(NB,128)) for c in range(NB)]
@@ -117,11 +116,11 @@
 
 
 def pair_kernel(
-    pairs, slot_ref, first_ref, second_ref, kept_out, came_out,
-    kept, came, leaving, gram_out, gram_in, cross_out, cross_in, diag_out, diag_in, diag_kept, turn,
+    pairs, slot_ref, order_ref, hessian_ref, kept_out, came_out,
+    slab, turned, kept, came, leaving, gram_out, gram_in, cross_out, cross_in, diag_out, diag_in, diag_kept, turn,
     g_ref, a_ref, e_ref,
     gram_sent, gram_came, cross_sent, cross_came, diag_sent, diag_came, turn_sent, turn_came,
-    block_sent, block_came, local_sem,
+    block_sent, block_came, load_sem, local_sem,
 ):
     row = lax.axis_index("row")
     col = lax.axis_index("col")
@@ -141,18 +140,34 @@
         stride = (step * step * step + 5 * step + 6) // 6
         return col + stride * (1 - 2 * ((col // stride) % 2))
 
+    chunk = turned.shape[2]
+    chunks = slab.shape[0] // chunk
+
+    def load(index):
+        rows = pl.ds(pl.multiple_of(index * chunk, chunk), chunk)
+        return pltpu.make_async_copy(hessian_ref.at[rows], slab.at[rows], load_sem.at[index])
+
+    for index in range(chunks):
+        load(index).start()
+
     barrier = pltpu.get_barrier_semaphore()
     for shift in range(1, pairs):
         pl.semaphore_signal(barrier, inc=1, device_id=((row + shift) % pairs, col), device_id_type=MESH)
     for step in range(STEPS):
         pl.semaphore_signal(barrier, inc=1, device_id=(row, partner(step)), device_id_type=MESH)
 
-    load_first = pltpu.make_async_copy(first_ref, kept, local_sem.at[0])
-    load_second = pltpu.make_async_copy(second_ref, came.at[0], local_sem.at[1])
-    load_first.start()
-    load_second.start()
-    load_first.wait()
-    load_second.wait()
+    def gather(index, _):
+        load(index).wait()
+        rows = pl.ds(pl.multiple_of(index * chunk, chunk), chunk)
+        for part in range(slab.shape[1] // 384):
+            turned[4 * part : 4 * part + 4] = jnp.transpose(
+                slab[rows, 384 * part : 384 * part + 384]).reshape(4, BW, chunk)
+        for pair in range(pairs):
+            kept[pair, :, rows] = turned[order_ref[0, 2 * pair]]
+            came[0, pair, :, rows] = turned[order_ref[0, 2 * pair + 1]]
+        return 0
+
+    lax.fori_loop(0, chunks, gather, 0)
     pl.semaphore_wait(barrier, pairs - 1 + STEPS)
 
     def gram_copy(pair):
@@ -358,13 +373,17 @@
 
             own_rotation(step)
 
-            @pl.when(step < STEPS - 1)
-            def _():
-                own_diagonals(step)
-
-            for part in range(2):
+            def pass_on(part):
                 turn_arrival(step, part, beyond).wait_recv()
                 neighbours(lambda target: turn_copy(step, part, beyond, target).start())
+
+            pass_on(0)
+
+            @pl.when(step < STEPS - 1)
+            def _():
+                own_diagonals(step)
+
+            pass_on(1)
 
         def update_next(i, _):
             update_one(step, ordered(start, i))
@@ -387,34 +406,49 @@
 
     lax.fori_loop(0, 6, phase, 0)
 
-    store_kept = pltpu.make_async_copy(kept, kept_out, local_sem.at[0])
-    store_kept.start()
-
-    def finish(pair, _):
+    def store(which, pair, index):
+        source, target = ((kept.at[pair], kept_out), (came.at[STEPS, pair], came_out))[which]
+        rows = pl.ds(pl.multiple_of(index * chunk, chunk), chunk)
+        return pltpu.make_async_copy(source.at[:, rows], target.at[index, pair], local_sem.at[which, pair, index])
+
+    def each(function):
+        def one(i, _):
+            function(i // chunks, i % chunks)
+            return 0
+
+        lax.fori_loop(0, pairs * chunks, one, 0)
+
+    each(lambda pair, index: store(0, pair, index).start())
+
+    def finish(i, _):
+        pair = ordered(0, i)
         block_copy(STEPS - 1, pair).wait()
+        for index in range(chunks):
+            store(1, pair, index).start()
         return 0
 
     lax.fori_loop(0, pairs, finish, 0)
-    store_came = pltpu.make_async_copy(came.at[STEPS], came_out, local_sem.at[1])
-    store_came.start()
-    store_kept.wait()
-    store_came.wait()
-
-
-def pair_steps(send_slot, first, second):
-    pairs, width, rows = first.shape
-    block = jax.ShapeDtypeStruct(first.shape, F32)
+    for which in range(2):
+        each(lambda pair, index: store(which, pair, index).wait())
+
+
+def pair_steps(send_slot, block_order, hessian):
+    rows, columns = hessian.shape
+    pairs, width, chunk = columns // W, BW, 256
+    block = jax.ShapeDtypeStruct((rows // chunk, pairs, width, chunk), F32)
     dma = pltpu.SemaphoreType.DMA
     return pl.pallas_call(
         functools.partial(pair_kernel, pairs),
         out_shape=[block, block],
         in_specs=[
             pl.BlockSpec(memory_space=pltpu.SMEM),
-            pl.BlockSpec(memory_space=pl.ANY),
+            pl.BlockSpec(memory_space=pltpu.SMEM),
             pl.BlockSpec(memory_space=pl.ANY),
         ],
         out_specs=[pl.BlockSpec(memory_space=pl.ANY)] * 2,
         scratch_shapes=[
+            pltpu.VMEM((rows, columns), F32),
+            pltpu.VMEM((2 * pairs, width, chunk), F32),
             pltpu.VMEM((pairs, width, rows), F32),
             pltpu.VMEM((STEPS + 1, pairs, width, rows), F32),
             pltpu.VMEM((pairs, width, rows), F32),
@@ -439,63 +473,32 @@
             dma((STEPS, pairs, 2)),
             dma((pairs,)),
             dma((STEPS, pairs)),
-            dma((2,)),
+            dma((rows // chunk,)),
+            dma((2, pairs, rows // chunk)),
         ],
         compiler_params=pltpu.CompilerParams(
             collective_id=0, has_side_effects=True, vmem_limit_bytes=VMEM_LIMIT),
         name="pair_steps",
-    )(send_slot, first, second)
-
-
-def gather_kernel(order_ref, hessian_ref, first_ref, second_ref, turned):
-    chunk = hessian_ref.shape[0]
-    for part in range(hessian_ref.shape[1] // 384):
-        turned[4 * part : 4 * part + 4] = jnp.transpose(
-            hessian_ref[:, 384 * part : 384 * part + 384]).reshape(4, BW, chunk)
-    for pair in range(first_ref.shape[0]):
-        first_ref[pair] = turned[order_ref[0, 2 * pair]]
-        second_ref[pair] = turned[order_ref[0, 2 * pair + 1]]
-
-
-def gathered(hessian, block_order):
-    rows, columns = hessian.shape
-    blocks = columns // BW
-    chunk = 256
-    shape = jax.ShapeDtypeStruct((blocks // 2, BW, rows), F32)
-    spec = pl.BlockSpec((blocks // 2, BW, chunk), lambda i: (0, 0, i))
-    return pl.pallas_call(
-        gather_kernel,
-        grid=(rows // chunk,),
-        out_shape=[shape, shape],
-        in_specs=[
-            pl.BlockSpec(memory_space=pltpu.SMEM),
-            pl.BlockSpec((chunk, columns), lambda i: (i, 0)),
-        ],
-        out_specs=[spec, spec],
-        scratch_shapes=[pltpu.VMEM((blocks, BW, chunk), F32)],
-        compiler_params=pltpu.CompilerParams(vmem_limit_bytes=VMEM_LIMIT),
-        name="gathered",
-    )(block_order, hessian)
+    )(send_slot, block_order, hessian)
 
 
 def scatter_kernel(slot_ref, kept_ref, came_ref, out_ref):
-    for pair in range(0, kept_ref.shape[0], 2):
+    for pair in range(0, kept_ref.shape[1], 2):
         parts = []
         for each in (pair, pair + 1):
             came_first = slot_ref[STEPS - 1, each] == 0
-            kept, came = kept_ref[each], came_ref[each]
+            kept, came = kept_ref[0, each], came_ref[0, each]
             parts += [jnp.where(came_first, came, kept), jnp.where(came_first, kept, came)]
         out_ref[:, 192 * pair : 192 * pair + 384] = jnp.transpose(jnp.concatenate(parts, 0))
 
 
 def scattered(send_slot, kept, came):
-    pairs, width, rows = kept.shape
-    chunk = 256
-    spec = pl.BlockSpec((pairs, width, chunk), lambda i: (0, 0, i))
+    chunks, pairs, width, chunk = kept.shape
+    spec = pl.BlockSpec((1, pairs, width, chunk), lambda i: (i, 0, 0, 0))
     return pl.pallas_call(
         scatter_kernel,
-        grid=(rows // chunk,),
-        out_shape=jax.ShapeDtypeStruct((rows, pairs * 2 * width), F32),
+        grid=(chunks,),
+        out_shape=jax.ShapeDtypeStruct((chunks * chunk, pairs * 2 * width), F32),
         in_specs=[pl.BlockSpec(memory_space=pltpu.SMEM), spec, spec],
         out_specs=pl.BlockSpec((chunk, pairs * 2 * width), lambda i: (i, 0)),
         compiler_params=pltpu.CompilerParams(vmem_limit_bytes=VMEM_LIMIT),
@@ -504,8 +507,7 @@
 
 
 def body(hessian, block_order, send_slot):
-    first, second = gathered(hessian, block_order)
-    kept, came = pair_steps(send_slot, first, second)
+    kept, came = pair_steps(send_slot, block_order, hessian)
     return scattered(send_slot, kept, came)
 
 

time: 300 us -> 293 us (0.977)
  Pallas kernels: 299 us -> 292 us
    pallas_call x2 -> x1, Pallas kernels: 13.4 us -> 6.54 us  [scattered(): pl.pallas_call(scatter_kernel, grid=(chunks,), out_shape=jax.ShapeDtypeSt...]
where the time goes in v8:
time: 293 us; the launch traced here: 292 us
  Pallas kernels  292 us (100%)
    pallas_call x1, Pallas kernels, pair_steps(): pl.pallas_call(functools.partial(pair_kernel, pairs), out_shape=[block, b...  285 us
    pallas_call x1, Pallas kernels, scattered(): pl.pallas_call(scatter_kernel, grid=(chunks,), out_shape=jax.ShapeDtypeSt...  6.54 us

profile of v8, /device:TPU:0, one launch (start us, length us, event | category | flops | bytes accessed | tf_op | source)
XLA Modules:
  0.0 291.6 jit_solution(14858222371136409670)
XLA Ops:
  0.0 285.1 %pair_steps.1 = (f32[4,8,96,256]{3,2,1,0:T(8,128)}, f32[4,8,96,256]{3,2,1,0:T(8,128)}) custom-call(s32[4,8]{1,0:T(4,128)} %slot_ref.3, s32[1,16]{1,0:T(1,128)} %order_ref.1, f32[1024,1536]{1,0:T(8,128)} %hessian_ref.1), custom_call_target="tpu_custom_call" | custom-call | tf_op jit(solution)/shard_map/pair_steps/pallas_call | solution.py:440
  285.1 6.5 %scattered.1 = f32[1024,1536]{1,0:T(8,128)} custom-call(s32[4,8]{1,0:T(4,128)} %slot_ref.3, f32[4,8,96,256]{3,2,1,0:T(8,128)} %get-tuple-element.7.kept_ref, f32[4,8,96,256]{3,2,1,0:T(8,128)} %get-tuple-element.8.came_ref), custom_call_target="tpu_custom_call" | custom-call | tf_op jit(solution)/shard_map/scattered/pallas_call | solution.py:498

commit v9 on v8

--- a/solution.py
+++ b/solution.py
@@ -8,7 +8,6 @@
 from jax.sharding import PartitionSpec as P
 
 MESH = pl.DeviceIdType.MESH
-
 F32=jnp.float32; BF=jnp.bfloat16
 W=192;BW=96
 def pieces(x):
@@ -337,7 +336,10 @@
             + lax.dot_general(turn_high, high, dims, preferred_element_type=F32))
         kept[pair] = new[0:BW]
         leaving[pair] = new[BW:]
-        block_copy(step, pair).start()
+
+        @pl.when((step != 1) | (pair < half))
+        def _():
+            block_copy(step, pair).start()
 
     def phase(index, _):
         split = jnp.minimum(index // 2, 1)
@@ -360,6 +362,14 @@
             return 0
 
         lax.fori_loop(0, count, gram_one, 0)
+
+        @pl.when((step == 2) & (start == 0))
+        def _():
+            def held_back(i, _):
+                block_copy(1, ordered(half, i)).start()
+                return 0
+
+            lax.fori_loop(0, half, held_back, 0)
 
         @pl.when(mine)
         def _():

time: 293 us -> 291 us (level)
  no operation moved by 1% of the time
where the time goes in v9:
time: 291 us; the launch traced here: 290 us
  Pallas kernels  290 us (100%)
    pallas_call x1, Pallas kernels, pair_steps(): pl.pallas_call(functools.partial(pair_kernel, pairs), out_shape=[block, b...  284 us
    pallas_call x1, Pallas kernels, scattered(): pl.pallas_call(scatter_kernel, grid=(chunks,), out_shape=jax.ShapeDtypeSt...  6.54 us

profile of v9, /device:TPU:0, one launch (start us, length us, event | category | flops | bytes accessed | tf_op | source)
XLA Modules:
  0.0 290.3 jit_solution(15218192206089191264)
XLA Ops:
  0.0 283.8 %pair_steps.1 = (f32[4,8,96,256]{3,2,1,0:T(8,128)}, f32[4,8,96,256]{3,2,1,0:T(8,128)}) custom-call(s32[4,8]{1,0:T(4,128)} %slot_ref.3, s32[1,16]{1,0:T(1,128)} %order_ref.1, f32[1024,1536]{1,0:T(8,128)} %hessian_ref.1), custom_call_target="tpu_custom_call" | custom-call | tf_op jit(solution)/shard_map/pair_steps/pallas_call | solution.py:450
  283.8 6.5 %scattered.1 = f32[1024,1536]{1,0:T(8,128)} custom-call(s32[4,8]{1,0:T(4,128)} %slot_ref.3, f32[4,8,96,256]{3,2,1,0:T(8,128)} %get-tuple-element.7.kept_ref, f32[4,8,96,256]{3,2,1,0:T(8,128)} %get-tuple-element.8.came_ref), custom_call_target="tpu_custom_call" | custom-call | tf_op jit(solution)/shard_map/scattered/pallas_call | solution.py:508
